TPU v7x, 32 devices: a whole 2x2x4 slice. The times are simulated.
32 devices in a mesh: dp: 4 (over y, core), ctx: 8 (over z, x).
Axes of the slice: x: 2, y: 2, z: 4, core: 2. Of those that a mesh axis runs over, the one named last changes fastest.
Arguments:
- queries: bfloat16 [4096, 2048], P(('dp', 'ctx')), parts along dimension 0, may hold values from -9 to 9
- keys: bfloat16 [4096, 512], P(('dp', 'ctx')), parts along dimension 0, may hold values from -9 to 9
- values: bfloat16 [4096, 512], P(('dp', 'ctx')), parts along dimension 0, may hold values from -6 to 6
- grad_out: bfloat16 [4096, 2048], P(('dp', 'ctx')), parts along dimension 0, may hold values from -6 to 6
- positions: int32 [1024], P('dp'), parts along dimension 0, may hold values from 0 to 1023, as said below
Outputs:
- attended: bfloat16 [4096, 2048], P(('dp', 'ctx')), parts along dimension 0
- grad_queries: bfloat16 [4096, 2048], P(('dp', 'ctx')), parts along dimension 0
- grad_keys: bfloat16 [4096, 512], P(('dp', 'ctx')), parts along dimension 0
- grad_values: bfloat16 [4096, 512], P(('dp', 'ctx')), parts along dimension 0
There are 4 independent parts, one for each index of `dp`. A program takes and returns all parts, laid end to end along the dimension named above; each array names one. Nothing has to cross between parts.
Inputs may be any that keep to these rules, and one draw needn't show every extreme that they name: 256 distinct token positions in increasing order; the 128 tokens of one index of ctx hold at most 32 of them, and one index holds exactly 32.
All inputs are finite; a program needn't handle non-finite values.
Results may differ from a plain program's by a relative error of at most 0.0075.
Values may be sent and summed in bfloat16 or wider, within the bound.
A program may use at most 192 MiB of HBM per device.

v0:
```python
import math

import jax
import jax.numpy as jnp
from jax import lax
from jax.sharding import PartitionSpec as P

HQ = 16
HK = 4
DH = 128
BLOCK = 64
CAP = 32


highest = lax.Precision.HIGHEST


def with_halo(array, sides, width):
    for axis, dim in sides:
        size, length = (lax.axis_size(axis), array.shape[dim])
        up = [(i, (i + 1) % size) for i in range(size - 1)]
        down = [(j, i) for i, j in up]
        last = lax.slice_in_dim(array, length - width, length, axis=dim)
        first = lax.slice_in_dim(array, 0, width, axis=dim)
        before = lax.ppermute(last, axis, up)
        after = lax.ppermute(first, axis, down)
        array = jnp.concatenate([before, array, after], axis=dim)
    return array


def combined_all(part, axis, combine):
    gathered = jax.tree.map(lambda a: lax.all_gather(a, axis), part)

    def take(source):
        return jax.tree.map(lambda a: lax.dynamic_index_in_dim(a, source, 0, False), gathered)

    return lax.fori_loop(
        1, lax.axis_size(axis), lambda source, state: combine(state, take(source)), take(0)
    )


def window_group(pieces, glob_keys, glob_values, score_scale):
    query_block, grad_block, key_window, value_window, key_usable, query_live = pieces
    near = (
        jnp.einsum("bqard,bkad->barqk", query_block, key_window, preferred_element_type=jnp.float32)
        * score_scale
    )
    far = (
        jnp.einsum("bqard,gad->barqg", query_block, glob_keys, preferred_element_type=jnp.float32)
        * score_scale
    )
    near = jnp.where(key_usable[:, None, None, None, :], near, -jnp.inf)
    row_top = jnp.maximum(jnp.max(near, axis=-1), jnp.max(far, axis=-1))
    near_weight = jnp.exp(near - row_top[..., None])
    far_weight = jnp.exp(far - row_top[..., None])
    total = jnp.sum(near_weight, axis=-1) + jnp.sum(far_weight, axis=-1)
    mixed = jnp.einsum(
        "barqk,bkad->bqard",
        near_weight.astype(jnp.bfloat16),
        value_window,
        preferred_element_type=jnp.float32,
    )
    mixed = mixed + jnp.einsum(
        "barqg,gad->bqard",
        far_weight.astype(jnp.bfloat16),
        glob_values,
        preferred_element_type=jnp.float32,
    )
    attended = mixed / jnp.transpose(total, (0, 3, 1, 2))[..., None]
    delta = jnp.transpose(jnp.sum(grad_block * attended, axis=-1), (0, 2, 3, 1))
    live = query_live[:, None, None, :, None]
    near_prob = near_weight / total[..., None]
    far_prob = far_weight / total[..., None]
    near_dprob = jnp.einsum(
        "bqard,bkad->barqk", grad_block, value_window, preferred_element_type=jnp.float32
    )
    far_dprob = jnp.einsum(
        "bqard,gad->barqg", grad_block, glob_values, preferred_element_type=jnp.float32
    )
    near_dscore = (near_prob * (near_dprob - delta[..., None]) * live).astype(jnp.bfloat16)
    far_dscore = (far_prob * (far_dprob - delta[..., None]) * live).astype(jnp.bfloat16)
    near_round = (near_prob * live).astype(jnp.bfloat16)
    far_round = (far_prob * live).astype(jnp.bfloat16)
    grad_query = jnp.einsum(
        "barqk,bkad->bqard", near_dscore, key_window, preferred_element_type=jnp.float32
    )
    grad_query = score_scale * (
        grad_query
        + jnp.einsum("barqg,gad->bqard", far_dscore, glob_keys, preferred_element_type=jnp.float32)
    )
    grad_key_win = score_scale * jnp.einsum(
        "barqk,bqard->bkad", near_dscore, query_block, preferred_element_type=jnp.float32
    )
    grad_value_win = jnp.einsum(
        "barqk,bqard->bkad", near_round, grad_block, preferred_element_type=jnp.float32
    )
    grad_key_glob = score_scale * jnp.einsum(
        "barqg,bqard->gad", far_dscore, query_block, preferred_element_type=jnp.float32
    )
    grad_value_glob = jnp.einsum(
        "barqg,bqard->gad", far_round, grad_block, preferred_element_type=jnp.float32
    )
    return (attended, grad_query, grad_key_win, grad_value_win, grad_key_glob, grad_value_glob)


def combine_softmax(left_part, right_part):
    left_top, left_total, left_summed = left_part
    right_top, right_total, right_summed = right_part
    joint_top = jnp.maximum(left_top, right_top)
    left_factor = jnp.exp(left_top - joint_top)
    right_factor = jnp.exp(right_top - joint_top)
    return (
        joint_top,
        left_total * left_factor + right_total * right_factor,
        left_summed * left_factor[..., None] + right_summed * right_factor[..., None],
    )


def local(queries, keys, values, grad_out, positions):
    tok_rows = queries.shape[0]
    query_width = queries.shape[1]
    key_width = keys.shape[1]
    q_per_kv = HQ // HK
    ctx_count = lax.axis_size("ctx")
    seq_total = tok_rows * ctx_count
    first_row = lax.axis_index("ctx") * tok_rows
    score_scale = 1.0 / math.sqrt(DH)
    glob_count = positions.shape[0]
    local_row = positions - first_row
    is_mine = (local_row >= 0) & (local_row < tok_rows)
    safe_row = jnp.clip(local_row, 0, tok_rows - 1)
    before = jnp.sum((positions < first_row).astype(jnp.int32))
    held_count = jnp.sum(is_mine.astype(jnp.int32))
    slot_index = jnp.arange(CAP)
    slot_ok = slot_index < held_count
    slot_row = jnp.clip(
        positions[jnp.clip(before + slot_index, 0, glob_count - 1)] - first_row, 0, tok_rows - 1
    )
    owner_index = positions // tok_rows
    owner_start = jnp.sum((owner_index[None, :] < owner_index[:, None]).astype(jnp.int32), axis=1)
    slot_of = owner_index * CAP + jnp.arange(glob_count) - owner_start
    packed = jnp.concatenate(
        [queries[slot_row], keys[slot_row], values[slot_row], grad_out[slot_row]], axis=1
    )
    packed = jnp.where(slot_ok[:, None], packed, jnp.zeros_like(packed))
    everyone = lax.all_gather(packed, "ctx", axis=0, tiled=True)
    compact = everyone[slot_of]
    glob_query = compact[:, :query_width].reshape(glob_count, HK, q_per_kv, DH)
    glob_keys = compact[:, query_width : query_width + key_width].reshape(glob_count, HK, DH)
    glob_values = compact[:, query_width + key_width : query_width + 2 * key_width].reshape(
        glob_count, HK, DH
    )
    glob_grad = compact[:, query_width + 2 * key_width :].reshape(glob_count, HK, q_per_kv, DH)
    paired = jnp.concatenate([keys, values], axis=1)
    extended = with_halo(paired, (("ctx", 0),), BLOCK)
    blocks = tok_rows // BLOCK
    ext_blocks = extended.reshape(blocks + 2, BLOCK, 2 * key_width)
    window = jnp.concatenate([ext_blocks[:-2], ext_blocks[1:-1], ext_blocks[2:]], axis=1)
    key_window = window[:, :, :key_width].reshape(blocks, 3 * BLOCK, HK, DH)
    value_window = window[:, :, key_width:].reshape(blocks, 3 * BLOCK, HK, DH)
    ext_position = first_row - BLOCK + jnp.arange(tok_rows + 2 * BLOCK)
    ext_global = jnp.any(ext_position[:, None] == positions[None, :], axis=1)
    ext_usable = (
        (ext_position >= 0) & (ext_position < seq_total) & jnp.logical_not(ext_global)
    ).reshape(blocks + 2, BLOCK)
    key_usable = jnp.concatenate([ext_usable[:-2], ext_usable[1:-1], ext_usable[2:]], axis=1)
    query_live = (
        jnp.logical_not(ext_global[BLOCK : BLOCK + tok_rows])
        .astype(jnp.float32)
        .reshape(blocks, BLOCK)
    )
    per_step = min(8, blocks)
    step_count = blocks // per_step

    def regroup(source):
        return source.reshape((step_count, per_step) + source.shape[1:])

    stacked = (
        regroup(queries.reshape(blocks, BLOCK, HK, q_per_kv, DH)),
        regroup(grad_out.reshape(blocks, BLOCK, HK, q_per_kv, DH)),
        regroup(key_window),
        regroup(value_window),
        regroup(key_usable),
        regroup(query_live),
    )
    results = lax.map(
        lambda pieces: window_group(pieces, glob_keys, glob_values, score_scale), stacked
    )
    attended_loc = results[0].reshape(tok_rows, query_width)
    grad_query_loc = results[1].reshape(tok_rows, query_width)
    window_grads = jnp.concatenate(
        [
            results[2].reshape(blocks, 3, BLOCK, key_width),
            results[3].reshape(blocks, 3, BLOCK, key_width),
        ],
        axis=3,
    )
    glob_key_grad = jnp.sum(results[4], axis=0).reshape(glob_count, key_width)
    glob_value_grad = jnp.sum(results[5], axis=0).reshape(glob_count, key_width)
    key_here = keys.reshape(tok_rows, HK, DH)
    value_here = values.reshape(tok_rows, HK, DH)
    glob_score = (
        jnp.einsum("gard,uad->argu", glob_query, key_here, preferred_element_type=jnp.float32)
        * score_scale
    )
    top_here = jnp.max(glob_score, axis=-1)
    weight_here = jnp.exp(glob_score - top_here[..., None])
    total_here = jnp.sum(weight_here, axis=-1)
    summed_here = jnp.einsum(
        "argu,uad->argd", weight_here, value_here.astype(jnp.float32), precision=highest
    )
    glob_top, glob_total, glob_summed = combined_all(
        (top_here, total_here, summed_here), "ctx", combine_softmax
    )
    glob_attended = glob_summed / glob_total[..., None]
    glob_delta = jnp.sum(
        jnp.transpose(glob_grad, (1, 2, 0, 3)).astype(jnp.float32) * glob_attended, axis=-1
    )
    glob_prob = jnp.exp(glob_score - glob_top[..., None]) / glob_total[..., None]
    glob_dprob = jnp.einsum(
        "gard,uad->argu", glob_grad, value_here, preferred_element_type=jnp.float32
    )
    glob_dscore = (glob_prob * (glob_dprob - glob_delta[..., None])).astype(jnp.bfloat16)
    glob_round = glob_prob.astype(jnp.bfloat16)
    glob_query_grad = score_scale * jnp.einsum(
        "argu,uad->gard", glob_dscore, key_here, preferred_element_type=jnp.float32
    )
    key_grad_here = score_scale * jnp.einsum(
        "argu,gard->uad", glob_dscore, glob_query, preferred_element_type=jnp.float32
    )
    value_grad_here = jnp.einsum(
        "argu,gard->uad", glob_round, glob_grad, preferred_element_type=jnp.float32
    )
    empty_block = jnp.zeros((1, BLOCK, 2 * key_width), jnp.float32)
    spread = jnp.concatenate([window_grads[:, 0], empty_block, empty_block], axis=0)
    spread = spread + jnp.concatenate([empty_block, window_grads[:, 1], empty_block], axis=0)
    spread = spread + jnp.concatenate([empty_block, empty_block, window_grads[:, 2]], axis=0)
    rims = jnp.concatenate([spread[0], spread[-1]], axis=0)
    arrived = with_halo(rims, (("ctx", 0),), BLOCK)
    pair_grad = spread[1:-1].reshape(tok_rows, 2 * key_width)
    pair_grad = pair_grad.at[:BLOCK].add(arrived[:BLOCK])
    pair_grad = pair_grad.at[tok_rows - BLOCK :].add(arrived[3 * BLOCK :])
    pair_grad = pair_grad + jnp.concatenate(
        [key_grad_here.reshape(tok_rows, key_width), value_grad_here.reshape(tok_rows, key_width)],
        axis=1,
    )
    glob_grads = jnp.concatenate(
        [glob_query_grad.reshape(glob_count, query_width), glob_key_grad, glob_value_grad], axis=1
    )
    laid = (
        jnp.zeros((ctx_count * CAP, glob_grads.shape[1]), jnp.float32).at[slot_of].set(glob_grads)
    )
    returned = lax.psum_scatter(laid, "ctx", scatter_dimension=0, tiled=True)
    target = jnp.where(slot_ok, slot_row, tok_rows)
    grad_query_all = grad_query_loc.at[target].add(returned[:, :query_width], mode="drop")
    pair_grad = pair_grad.at[target].add(returned[:, query_width:], mode="drop")
    glob_rows_out = jnp.transpose(glob_attended, (2, 0, 1, 3)).reshape(glob_count, query_width)
    attended_all = attended_loc.at[jnp.where(is_mine, safe_row, tok_rows)].set(
        glob_rows_out, mode="drop"
    )
    return (
        attended_all.astype(jnp.bfloat16),
        grad_query_all.astype(jnp.bfloat16),
        pair_grad[:, :key_width].astype(jnp.bfloat16),
        pair_grad[:, key_width:].astype(jnp.bfloat16),
    )


def solution(mesh):
    in_specs = (
        P(("dp", "ctx"), None),
        P(("dp", "ctx"), None),
        P(("dp", "ctx"), None),
        P(("dp", "ctx"), None),
        P("dp"),
    )
    out_specs = (
        P(("dp", "ctx"), None),
        P(("dp", "ctx"), None),
        P(("dp", "ctx"), None),
        P(("dp", "ctx"), None),
    )
    return jax.shard_map(local, mesh=mesh, in_specs=in_specs, out_specs=out_specs, check_vma=False)
```

profile of v0, /device:TPU:0, one launch (start us, length us, event | category | flops | bytes accessed | tf_op | source)
XLA Modules:
  0.0 453.2 jit_solution(16199911689544137280)
XLA Ops:
  7.2 1.9 convert_reduce_fusion.1
  9.8 1.4 gather_fusion
  11.9 1.2 fusion.90
  13.1 1.9 gather_fusion.1
  18.8 56.4 %all-gather.6.cloned.1.call-done = bf16[256,5120]{1,0:T(8,128)(2,1)} async-done(((bf16[32,5120]{1,0:T(8,128)(2,1)}), bf16[256,5120]{1,0:T(8,128)(2,1)}) %all-gather.6.cloned.1.call-update) | async-done | bytes 2621456 | tf_op jit(solution)/shard_map/all_gather | solution.py:146
  75.3 6.8 %gather_fusion.5 = bf16[256,5120]{1,0:T(8,128)(2,1)S(1)} fusion(bf16[256,5120]{1,0:T(8,128)(2,1)} %all-gather.6.cloned.1.call-done, s32[1024]{0:T(1024)S(1)} %pad_clamp_fusion), kind=kCustom, calls=%fused_computation.5 | custom fusion | bytes 5243904 | tf_op jit(solution)/shard_map/gather | solution.py:147
  82.0 1.6 fusion.98
  84.2 1.5 copy.209
  86.8 3.2 fusion.23
  91.8 3.1 collective-permute-start
  94.9 1.3 collective-permute-start.1
  97.6 1.2 squeeze.82
  98.8 1.2 squeeze.86
  100.7 2.5 collective-permute-done.1
  105.1 1.1 squeeze.81
  107.1 2.4 bitcast_reduce_fusion.2
  109.9 31.6 %all-gather.1 = f32[32,4,256]{2,1,0:T(4,128)S(1)} all-gather(f32[4,4,256]{2,1,0:T(4,128)S(1)} %fusion.25), channel_id=3, replica_groups=mesh['dp'=4,'ctx'=8] {'ctx'}, dimensions={0}, use_global_device_ids=true | all-gather | bytes 147456 | tf_op jit(solution)/shard_map/all_gather | solution.py:32
  141.5 31.7 %all-gather = f32[32,4,256]{2,1,0:T(4,128)S(1)} all-gather(f32[4,4,256]{2,1,0:T(4,128)S(1)} %copy-done.35), channel_id=2, replica_groups=mesh['dp'=4,'ctx'=8] {'ctx'}, dimensions={0}, use_global_device_ids=true | all-gather | bytes 147456 | tf_op jit(solution)/shard_map/all_gather | solution.py:32
  173.9 2.3 copy.227
  176.2 1.1 fusion.99
  183.3 1.6 multiply_reduce_fusion
  185.9 1.2 fusion.37
  187.1 2.0 copy.238
  189.1 2.2 fusion.44
  191.3 2.1 copy.239
  193.4 125.3 %all-gather.8.cloned.1.call-done = f32[32,4,256,128]{3,2,1,0:T(8,128)} async-done(((f32[4,4,256,128]{3,2,1,0:T(8,128)}), f32[32,4,256,128]{3,2,1,0:T(8,128)}) %all-gather.8.cloned.1.call-update) | async-done | bytes 16777232 | tf_op jit(solution)/shard_map/all_gather | solution.py:32
  318.7 1.7 slice.196
  320.4 24.4 %while.14 = (s32[]{:T(128)}, f32[4,4,256]{2,1,0:T(4,128)S(1)}, f32[4,4,256]{2,1,0:T(4,128)S(1)}, f32[4,4,256,128]{3,2,1,0:T(8,128)S(1)}, f32[8,4,4,256]{3,2,1,0:...) while((s32[]{:T(128)}, f32[4,4,256]{2,1,0:T(4,128)S(1)}, ...), condition=%wide.region_11.12_spmd, body=%wide.region_10.11_spmd.sunk | while | flops 1597445 | bytes 6455447 | solution.py:37
  321.2 2.7 fusion.128
  324.7 2.7 fusion.128
  328.2 2.7 fusion.128
  331.7 2.7 fusion.128
  335.2 2.7 fusion.128
  338.7 2.7 fusion.128
  342.2 2.7 fusion.128
  344.9 1.8 copy.214
  346.7 3.7 fusion.9
  352.2 1.8 convolution_multiply_fusion
  353.9 2.9 copy.237
  356.9 5.8 %scatter_custom_fusion.1 = f32[256,3072]{1,0:T(8,128)} fusion(s32[256]{0:T(256)} %copy-done.42, f32[256,512]{1,0:T(8,128)} %copy.239, f32[]{:T(128)} %constant.189.clone.1, f32[256,512]{1,0:T(8,128)} %copy.238, f32[256,2048]{1,0:T(8,128)} %copy.237, f32[]{:T(128)} %constant.198.clone.1), kind=kCustom, calls=%fused_computation.18 | custom fusion | flops 1572864 | bytes 6292480 | tf_op jit(solution)/shard_map/scatter | solution.py:251
  362.7 2.8 fusion.17
  366.5 1.4 copy.241
  367.9 1.5 reshape.271
  369.3 3.0 convolution_bitcast_fusion.4
  372.4 1.4 copy.243
  373.8 2.3 reshape.272
  376.2 1.1 copy-done.16
  378.5 3.3 collective-permute-start.2
  381.8 1.3 collective-permute-start.3
  385.5 1.4 reshape.266
  386.9 2.9 copy.208
  389.8 1.7 reshape.261
  391.5 5.0 %collective-permute-done.2 = f32[64,1024]{1,0:T(8,128)} collective-permute-done((f32[64,1024]{1,0:T(8,128)}, f32[64,1024]{1,0:T(8,128)}, u32[]{:S(2)}, u32[]{:S(2)}) %collective-permute-start.2) | collective-permute-done | bytes 262176 | tf_op jit(solution)/shard_map/ppermute | solution.py:25
  396.5 1.8 fusion.76
  398.2 1.8 fusion.74
  400.0 2.6 fusion.47
  402.6 1.1 copy.249
  403.7 2.0 fusion.38
  406.6 1.9 copy.215
  408.5 2.2 scatter_fusion
  411.6 1.3 maximum_add_fusion.1
  412.9 29.2 %reduce-scatter.2.cloned.1.call-done = f32[32,3072]{1,0:T(8,128)} async-done(((f32[256,3072]{1,0:T(8,128)}), f32[32,3072]{1,0:T(8,128)}) %reduce-scatter.2.cloned.1.call-update) | async-done | bytes 393232 | tf_op jit(solution)/shard_map/reduce_scatter | solution.py:253
  442.1 1.4 scatter_custom_fusion.3
  444.3 1.5 scatter_custom_fusion.2
  (167 shorter events, 36.4 us)
Async XLA Ops:
  7.2 7.8 %copy-start.8 = (bf16[128,2048]{1,0:T(8,128)(2,1)S(1)}, bf16[128,2048]{1,0:T(8,128)(2,1)}, u32[]{:S(2)}) copy-start(bf16[128,2048]{1,0:T(8,128)(2,1)} %param.14) | copy-start | bytes 1572868
  7.2 8.4 %copy-start.17 = (bf16[128,512]{1,0:T(8,128)(2,1)S(1)}, bf16[128,512]{1,0:T(8,128)(2,1)}, u32[]{:S(2)}) copy-start(bf16[128,512]{1,0:T(8,128)(2,1)} %param.12) | copy-start | bytes 393220
  7.2 9.1 %copy-start.18 = (bf16[128,512]{1,0:T(8,128)(2,1)S(1)}, bf16[128,512]{1,0:T(8,128)(2,1)}, u32[]{:S(2)}) copy-start(bf16[128,512]{1,0:T(8,128)(2,1)} %param.13) | copy-start | bytes 393220
  7.2 68.1 %all-gather.6.cloned.1.call-start = ((), (), s32[]{:S(2)}) async-start(), calls=%async_computation.1 | async-start | bytes 2949120 | tf_op jit(solution)/shard_map/all_gather | solution.py:146
  17.8 300.9 %all-gather.8.cloned.1.call-start = ((), (), s32[]{:S(2)}) async-start(), calls=%async_computation.3 | async-start | bytes 18874368 | tf_op jit(solution)/shard_map/all_gather | solution.py:32
  17.9 68.3 %copy-start.27 = (bf16[128,4,128]{2,1,0:T(4,128)(2,1)}, bf16[128,4,128]{2,1,0:T(4,128)(2,1)S(1)}, u32[]{:S(2)}) copy-start(bf16[128,4,128]{2,1,0:T(4,128)(2,1)S(1)} %reshape.264) | copy-start | bytes 393220
  18.0 67.6 %copy-start.20 = (bf16[128,4,128,1]{0,2,3,1:T(8,128)(2,1)}, bf16[128,4,128,1]{0,2,3,1:T(8,128)(2,1)S(1)}, u32[]{:S(2)}) copy-start(bf16[128,4,128,1]{0,2,3,1:T(8,128)(2,1)S(1)} %copy.266) | copy-start | bytes 393220
  18.2 0.6 copy-start.42
  82.0 2.1 copy-start.3
  85.6 1.0 copy-start.4
  86.2 0.6 copy-start.34
  86.2 23.3 %copy-start.1 = (f32[4,256,4,128]{1,3,2,0:T(8,128)}, f32[4,256,4,128]{1,3,2,0:T(8,128)S(1)}, u32[]{:S(2)}) copy-start(f32[4,256,4,128]{1,3,2,0:T(8,128)S(1)} %get-tuple-element.307) | copy-start | bytes 6291460
  90.0 6.2 %copy-start = (s32[256]{0:T(256)S(1)}, s32[256]{0:T(256)}, u32[]{:S(2)}) copy-start(s32[256]{0:T(256)} %param.15) | copy-start | bytes 3076
  90.0 7.6 %copy-start.7 = (bf16[128,2048]{1,0:T(8,128)(2,1)S(1)}, bf16[128,2048]{1,0:T(8,128)(2,1)}, u32[]{:S(2)}) copy-start(bf16[128,2048]{1,0:T(8,128)(2,1)} %param.11) | copy-start | bytes 1572868
  90.0 8.8 %copy-start.9 = (bf16[128,2048]{1,0:T(8,128)(2,1)S(1)}, bf16[128,2048]{1,0:T(8,128)(2,1)}, u32[]{:S(2)}) copy-start(bf16[128,2048]{1,0:T(8,128)(2,1)} %param.14) | copy-start | bytes 1572868
  90.0 352.1 %reduce-scatter.2.cloned.1.call-start = ((), (), s32[]{:S(2)}) async-start(), calls=%async_computation.2 | async-start | bytes 3538944 | tf_op jit(solution)/shard_map/reduce_scatter | solution.py:253
  91.8 8.9 %collective-permute-start = (bf16[64,1024]{1,0:T(8,128)(2,1)}, bf16[64,1024]{1,0:T(8,128)(2,1)}, u32[]{:S(2)}, u32[]{:S(2)}) collective-permute-start(bf16[64,1024]{1,0:T(8,128)(2,1)} %get-tuple-element.293), channel_id=1, source_target_pairs={{0,1},{1,2},{2,3},{3,4},{4,5},{5,6},{6,7},{8,9},{9,10},{10,11},{11... | collective-permute-start | bytes 393224 | tf_op jit(solution)/shard_map/ppermute | solution.py:25
  94.9 8.3 %collective-permute-start.1 = (bf16[64,1024]{1,0:T(8,128)(2,1)S(1)}, bf16[64,1024]{1,0:T(8,128)(2,1)}, u32[]{:S(2)}, u32[]{:S(2)}) collective-permute-start(bf16[64,1024]{1,0:T(8,128)(2,1)S(1)} %get-tuple-element.294), channel_id=1, source_target_pairs={{1,0},{2,1},{3,2},{4,3},{5,4},{6,5},{7,6},{9,8},{10,9},{11,10},{12... | collective-permute-start | bytes 393224 | tf_op jit(solution)/shard_map/ppermute | solution.py:26
  97.0 3.5 copy-start.43
  97.6 2.3 copy-start.45
  100.7 6.4 %copy-start.39 = (pred[2,192]{1,0:T(4,128)(4,1)}, pred[2,192]{1,0:T(4,128)(4,1)S(1)}, u32[]{:S(2)}) copy-start(pred[2,192]{1,0:T(4,128)(4,1)S(1)} %pad_add_fusion) | copy-start | bytes 1156
  104.2 2.9 copy-start.10
  106.2 3.3 copy-start.35
  141.5 32.3 %copy-start.31 = (f32[32,4,256]{2,1,0:T(4,128)}, f32[32,4,256]{2,1,0:T(4,128)S(1)}, u32[]{:S(2)}) copy-start(f32[32,4,256]{2,1,0:T(4,128)S(1)} %all-gather.1) | copy-start | bytes 393220
  173.2 0.7 copy-start.32
  177.2 1.5 copy-start.38
  178.2 2.2 copy-start.5
  178.2 2.2 copy-start.40
  178.8 183.9 %copy-start.30 = (f32[2,4,4,64]{3,2,1,0:T(4,128)}, f32[2,4,4,64]{3,2,1,0:T(4,128)S(1)}, u32[]{:S(2)}) copy-start(f32[2,4,4,64]{3,2,1,0:T(4,128)S(1)} %copy_maximum_fusion) | copy-start | bytes 24580
  178.8 2.6 copy-start.19
  181.3 0.8 copy-start.44
  181.4 181.3 %copy-start.37 = (f32[2,4,4,64]{3,2,1,0:T(4,128)}, f32[2,4,4,64]{3,2,1,0:T(4,128)S(1)}, u32[]{:S(2)}) copy-start(f32[2,4,4,64]{3,2,1,0:T(4,128)S(1)} %copy_add_fusion) | copy-start | bytes 24580
  182.1 1.1 copy-start.29
  182.2 1.2 copy-start.36
  185.9 5.4 %copy-start.22 = (bf16[2,4,4,64,256]{4,3,2,0,1:T(8,128)(2,1)}, bf16[2,4,4,64,256]{4,3,2,0,1:T(8,128)(2,1)S(1)}, u32[]{:S(2)}) copy-start(bf16[2,4,4,64,256]{4,3,2,0,1:T(8,128)(2,1)S(1)} %fusion.14) | copy-start | bytes 3145732
  193.4 127.1 %copy-start.24 = (f32[4,4,256]{2,1,0:T(4,128)S(1)}, f32[4,4,256]{2,1,0:T(4,128)}, u32[]{:S(2)}) copy-start(f32[4,4,256]{2,1,0:T(4,128)} %slice.194) | copy-start | bytes 49156
  344.9 5.6 %copy-start.25 = (f32[4,4,256]{2,1,0:T(4,128)}, f32[4,4,256]{2,1,0:T(4,128)S(1)}, u32[]{:S(2)}) copy-start(f32[4,4,256]{2,1,0:T(4,128)S(1)} %get-tuple-element.253) | copy-start | bytes 49156
  346.7 3.7 copy-start.2
  346.7 3.7 copy-start.11
  346.7 3.8 copy-start.28
  350.4 1.7 copy-start.21
  351.2 1.0 copy-start.12
  365.5 1.0 copy-start.14
  376.1 1.1 copy-start.16
  377.4 5.6 %copy-start.15 = (bf16[2,4,4,64,192]{4,3,2,1,0:T(8,128)(2,1)S(1)}, bf16[2,4,4,64,192]{4,3,2,1,0:T(8,128)(2,1)}, u32[]{:S(2)}) copy-start(bf16[2,4,4,64,192]{4,3,2,1,0:T(8,128)(2,1)} %copy-done.14) | copy-start | bytes 2359300
  377.6 6.4 %copy-start.6 = (f32[4,64,1024]{2,1,0:T(8,128)}, f32[4,64,1024]{2,1,0:T(8,128)S(1)}, u32[]{:S(2)}) copy-start(f32[4,64,1024]{2,1,0:T(8,128)S(1)} %fusion.43) | copy-start | bytes 3145732
  377.6 5.9 %copy-start.23 = (bf16[2,4,4,64,256]{4,3,2,0,1:T(8,128)(2,1)S(1)}, bf16[2,4,4,64,256]{4,3,2,0,1:T(8,128)(2,1)}, u32[]{:S(2)}) copy-start(bf16[2,4,4,64,256]{4,3,2,0,1:T(8,128)(2,1)} %copy-done.22) | copy-start | bytes 3145732
  378.5 18.0 %collective-permute-start.2 = (f32[64,1024]{1,0:T(8,128)}, f32[64,1024]{1,0:T(8,128)}, u32[]{:S(2)}, u32[]{:S(2)}) collective-permute-start(f32[64,1024]{1,0:T(8,128)} %get-tuple-element.286), channel_id=1, source_target_pairs={{0,1},{1,2},{2,3},{3,4},{4,5},{5,6},{6,7},{8,9},{9,10},{10,11},{11... | collective-permute-start | bytes 786440 | tf_op jit(solution)/shard_map/ppermute | solution.py:25
  381.8 16.5 %collective-permute-start.3 = (f32[64,1024]{1,0:T(8,128)}, f32[64,1024]{1,0:T(8,128)}, u32[]{:S(2)}, u32[]{:S(2)}) collective-permute-start(f32[64,1024]{1,0:T(8,128)} %get-tuple-element.285), channel_id=1, source_target_pairs={{1,0},{2,1},{3,2},{4,3},{5,4},{6,5},{7,6},{9,8},{10,9},{11,10},{12... | collective-permute-start | bytes 786440 | tf_op jit(solution)/shard_map/ppermute | solution.py:26
  389.8 10.2 %copy-start.26 = (f32[4,4,256]{2,1,0:T(4,128)S(1)}, f32[4,4,256]{2,1,0:T(4,128)}, u32[]{:S(2)}) copy-start(f32[4,4,256]{2,1,0:T(4,128)} %copy-done.25) | copy-start | bytes 49156
  406.5 1.9 copy-start.41
  411.6 32.7 %copy-start.13 = (f32[128,2048]{1,0:T(8,128)S(1)}, f32[128,2048]{1,0:T(8,128)}, u32[]{:S(2)}) copy-start(f32[128,2048]{1,0:T(8,128)} %reshape.266) | copy-start | bytes 3145732
  442.1 2.2 copy-start.33
Sparse Core Ops, SparseCore 0:
  17.9 57.3 all-gather.5
  90.1 228.5 all-gather.7
  362.8 79.2 reduce-scatter.1
where the time goes:
time: 455 us; the launch traced here: 453 us
  waiting for transfers between devices  219 us (48%)
  local copies, waits for them, and re-layouts  66.5 us (15%)
  blocking collectives  63.3 us (14%)
  other arithmetic  53.4 us (12%)
  matrix products  27.6 us (6%)
  between operations  14.5 us (3%)
  starting transfers between devices  9.09 us (2%)
    all_gather x1, waiting for transfers between devices, combined_all(): gathered = jax.tree.map(lambda a: lax.all_gather(a, axis), part)  125 us
    all_gather x2, blocking collectives, combined_all(): gathered = jax.tree.map(lambda a: lax.all_gather(a, axis), part)  63.3 us
    all_gather x1, waiting for transfers between devices, local(): everyone = lax.all_gather(packed, 'ctx', axis=0, tiled=True)  56.4 us
    reduce_scatter x1, waiting for transfers between devices, local(): returned = lax.psum_scatter(laid, 'ctx', scatter_dimension=0, tiled=True)  29.2 us
    add x7, other arithmetic, combine_softmax(): left_summed * left_factor[..., None]  18.8 us
  transfers between devices with their start and end apart: 7, of which 5 were waited for; matrix products, arithmetic and copies ran while one was open for 16% of the time, Pallas kernels for 0%

commit v1 on v0

--- a/solution.py
+++ b/solution.py
@@ -1,8 +1,11 @@
+import functools
 import math
 
 import jax
 import jax.numpy as jnp
 from jax import lax
+from jax.experimental import pallas as pl
+from jax.experimental.pallas import tpu as pltpu
 from jax.sharding import PartitionSpec as P
 
 HQ = 16
@@ -266,6 +269,393 @@
     )
 
 
+MESH = pl.DeviceIdType.MESH
+ROWS = 4
+REP = HQ // HK
+TOK = 128
+FAR = -1e30
+
+
+def dense_kernel(
+    pos_row, pos_col, q_ref, k_ref, v_ref, g_ref,
+    att_ref, gq_ref, gk_ref, gv_ref,
+    kbuf, vbuf, qt, gt, qs, gs, sbuf, dbuf, pbuf, wbuf, top8, inv, delta,
+    acc, xsend, xrecv, csend, crecv,
+    ax_s, ax_r, au_s, au_r, ad_s, ad_r, rx_s, rx_r, rc_s, rc_r,
+):
+    c = lax.axis_index("ctx")
+    z, x = c // 2, c % 2
+    partner = c + 1 - 2 * x
+    scale = 1.0 / math.sqrt(DH)
+    own = (k_ref, v_ref)
+    bufs = (kbuf, vbuf)
+    wide = REP * TOK
+
+    def rows(block):
+        return pl.ds(pl.multiple_of(block * TOK, TOK), TOK)
+
+    def head(j):
+        return pl.ds(pl.multiple_of(j * DH, DH), DH)
+
+    barrier = pltpu.get_barrier_semaphore()
+    pl.semaphore_signal(barrier, inc=1, device_id={"ctx": partner}, device_id_type=MESH)
+
+    @pl.when(z > 0)
+    def _():
+        pl.semaphore_signal(barrier, inc=1, device_id={"ctx": c - 2}, device_id_type=MESH)
+
+    @pl.when(z < ROWS - 1)
+    def _():
+        pl.semaphore_signal(barrier, inc=1, device_id={"ctx": c + 2}, device_id_type=MESH)
+
+    pl.semaphore_wait(
+        barrier, 1 + (z > 0).astype(jnp.int32) + (z < ROWS - 1).astype(jnp.int32)
+    )
+
+    def remote(source, target, send, recv, device):
+        return pltpu.make_async_remote_copy(
+            src_ref=source, dst_ref=target, send_sem=send, recv_sem=recv,
+            device_id={"ctx": device}, device_id_type=MESH,
+        )
+
+    def along(h, k, up, source=None):
+        block = c - 2 * (k - 1) if up else c + 2 * (k - 1)
+        here = bufs[h].at[rows(block)]
+        send, recv = (au_s, au_r) if up else (ad_s, ad_r)
+        return remote(
+            here if source is None else source, here,
+            send.at[h, k - 1], recv.at[h, k - 1], c + 2 if up else c - 2,
+        )
+
+    def along_in(h, k, up):
+        block = c - 2 * k if up else c + 2 * k
+        here = bufs[h].at[rows(block)]
+        send, recv = (au_s, au_r) if up else (ad_s, ad_r)
+        return remote(here, here, send.at[h, k - 1], recv.at[h, k - 1], partner)
+
+    def across(h, zz, source=None):
+        here = bufs[h].at[rows(2 * zz + x)]
+        return remote(
+            here if source is None else source, here, ax_s.at[h, zz], ax_r.at[h, zz], partner
+        )
+
+    def across_in(h, zz):
+        here = bufs[h].at[rows(2 * zz + 1 - x)]
+        return remote(here, here, ax_s.at[h, zz], ax_r.at[h, zz], partner)
+
+    for h in (0, 1):
+        across(h, z, own[h]).start()
+
+        @pl.when(z < ROWS - 1)
+        def _():
+            along(h, 1, True, own[h]).start()
+
+        @pl.when(z > 0)
+        def _():
+            along(h, 1, False, own[h]).start()
+
+    kbuf[rows(c), :] = k_ref[...]
+    vbuf[rows(c), :] = v_ref[...]
+
+    def stack(j, carry):
+        for r in range(REP):
+            cols = pl.ds(pl.multiple_of((j * REP + r) * DH, DH), DH)
+            part = q_ref[:, cols]
+            qs[j, r * TOK : (r + 1) * TOK, :] = part
+            qt[j, :, r * TOK : (r + 1) * TOK] = part.astype(jnp.float32).T.astype(jnp.bfloat16)
+            part = g_ref[:, cols]
+            gs[j, r * TOK : (r + 1) * TOK, :] = part
+            gt[j, :, r * TOK : (r + 1) * TOK] = part.astype(jnp.float32).T.astype(jnp.bfloat16)
+        return carry
+
+    lax.fori_loop(0, HK, stack, 0)
+    top8[...] = jnp.full(top8.shape, FAR, jnp.float32)
+
+    glob_count = pos_row.shape[1]
+    row_token = c * TOK + lax.broadcasted_iota(jnp.int32, (glob_count, TOK), 1)
+    row_glob = jnp.max(
+        jnp.where(pos_col[...] == row_token, 1.0, 0.0), axis=0, keepdims=True
+    )
+
+    def block_bias(block):
+        col_token = block * TOK + lax.broadcasted_iota(jnp.int32, (TOK, glob_count), 0)
+        col_glob = jnp.max(
+            jnp.where(pos_row[...] == col_token, 1.0, 0.0), axis=1, keepdims=True
+        )
+        u_block = block * (TOK // BLOCK) + lax.broadcasted_iota(jnp.int32, (TOK, TOK), 0) // BLOCK
+        t_block = c * (TOK // BLOCK) + lax.broadcasted_iota(jnp.int32, (TOK, TOK), 1) // BLOCK
+        near = jnp.where(jnp.abs(u_block - t_block) <= 1, 1.0, 0.0)
+        allowed = jnp.maximum(jnp.maximum(near, row_glob), col_glob)
+        bias = jnp.where(allowed > 0.5, 0.0, FAR)
+        return jnp.concatenate([bias] * REP, axis=1)
+
+    def scores(block):
+        bias = block_bias(block)
+        at = rows(block)
+
+        def one(j, carry):
+            s = jnp.dot(kbuf[at, head(j)], qt[j], preferred_element_type=jnp.float32)
+            s = s * scale + bias
+            sbuf[j, at, :] = s
+            top8[j] = jnp.maximum(top8[j], jnp.max(s.reshape(TOK // 8, 8, wide), axis=0))
+            dbuf[j, at, :] = jnp.dot(
+                vbuf[at, head(j)], gt[j], preferred_element_type=jnp.float32
+            )
+            return carry
+
+        lax.fori_loop(0, HK, one, 0)
+
+    scores(c)
+
+    def gather_step(k, carry):
+        @pl.when(z - k >= 0)
+        def _():
+            for h in (0, 1):
+                along_in(h, k, True).wait_recv()
+
+                @pl.when(z < ROWS - 1)
+                def _():
+                    along(h, k + 1, True).start()
+
+                across(h, z - k).start()
+
+        @pl.when(z + k < ROWS)
+        def _():
+            for h in (0, 1):
+                along_in(h, k, False).wait_recv()
+
+                @pl.when(z > 0)
+                def _():
+                    along(h, k + 1, False).start()
+
+                across(h, z + k).start()
+
+        @pl.when(z - k >= 0)
+        def _():
+            scores(c - 2 * k)
+
+        @pl.when(z + k < ROWS)
+        def _():
+            scores(c + 2 * k)
+
+        @pl.when(z - (k - 1) >= 0)
+        def _():
+            for h in (0, 1):
+                across_in(h, z - (k - 1)).wait_recv()
+            scores(2 * (z - (k - 1)) + 1 - x)
+
+        @pl.when((z + (k - 1) < ROWS) & (k > 1))
+        def _():
+            for h in (0, 1):
+                across_in(h, z + (k - 1)).wait_recv()
+            scores(2 * (z + (k - 1)) + 1 - x)
+
+        return carry
+
+    lax.fori_loop(1, ROWS + 1, gather_step, 0)
+
+    def stats(j, carry):
+        top = jnp.max(top8[j], axis=0, keepdims=True)
+
+        def part(b, sums):
+            total8, mixed8 = sums
+            at = rows(b)
+            e = jnp.exp(sbuf[j, at, :] - top)
+            sbuf[j, at, :] = e
+            total8 = total8 + jnp.sum(e.reshape(TOK // 8, 8, wide), axis=0)
+            e = e * dbuf[j, at, :]
+            return total8, mixed8 + jnp.sum(e.reshape(TOK // 8, 8, wide), axis=0)
+
+        zero = jnp.zeros((8, wide), jnp.float32)
+        total8, mixed8 = lax.fori_loop(0, 2 * ROWS, part, (zero, zero))
+        reciprocal = 1.0 / jnp.sum(total8, axis=0, keepdims=True)
+        inv[j] = jnp.broadcast_to(reciprocal, (8, wide))
+        delta[j] = jnp.broadcast_to(
+            jnp.sum(mixed8, axis=0, keepdims=True) * reciprocal, (8, wide)
+        )
+        return carry
+
+    lax.fori_loop(0, HK, stats, 0)
+
+    def terms(block, out):
+        at = rows(block)
+
+        def one(j, carry):
+            p = sbuf[j, at, :] * inv[j, 0:1, :]
+            w = (p * (dbuf[j, at, :] - delta[j, 0:1, :])).astype(jnp.bfloat16)
+            p = p.astype(jnp.bfloat16)
+            pbuf[j, at, :] = p
+            wbuf[j, at, :] = w
+            dk = jnp.dot(w, qs[j], preferred_element_type=jnp.float32) * scale
+            dv = jnp.dot(p, gs[j], preferred_element_type=jnp.float32)
+            out[0, :, head(j)] = dk.astype(out.dtype)
+            out[1, :, head(j)] = dv.astype(out.dtype)
+            return carry
+
+        lax.fori_loop(0, HK, one, 0)
+
+    def pick(a, b, d, e):
+        return jnp.where(z == 0, a, jnp.where(z == 1, b, jnp.where(z == 2, d, e)))
+
+    order = (pick(3, 3, 0, 0), pick(2, 0, 3, 1), pick(1, 2, 1, 2), z)
+
+    def cross(h, o):
+        return remote(
+            xsend.at[o, h], xrecv.at[o, h], rx_s.at[h, o], rx_r.at[h, o], partner
+        )
+
+    def phase(o):
+        terms(2 * order[o] + 1 - x, xsend.at[o])
+        for h in (0, 1):
+            cross(h, o).start()
+        terms(2 * order[o] + x, acc.at[o])
+
+    def chain(h, o):
+        down = order[o] < z
+        to = jnp.where(down, z - 1, z + 1)
+        slot = jnp.where((to == order[o]) & jnp.logical_not(down), ROWS, order[o])
+        return remote(
+            csend.at[o, h], crecv.at[slot, h], rc_s.at[h, o], rc_r.at[h, slot], 2 * to + x
+        )
+
+    def chain_in(h, slot):
+        return remote(crecv.at[slot, h], crecv.at[slot, h], rc_s.at[h, 0], rc_r.at[h, slot], partner)
+
+    def pass_on(o):
+        down = order[o] < z
+        fed = (down & (z < ROWS - 1)) | (jnp.logical_not(down) & (z > 0))
+        for h in (0, 1):
+            cross(h, o).wait_recv()
+            acc[o, h] = acc[o, h] + xrecv[o, h].astype(jnp.float32)
+
+            @pl.when(fed)
+            def _():
+                chain_in(h, order[o]).wait_recv()
+                acc[o, h] = acc[o, h] + crecv[order[o], h].astype(jnp.float32)
+
+            csend[o, h] = acc[o, h].astype(jnp.bfloat16)
+            chain(h, o).start()
+
+    phase(0)
+    phase(1)
+    phase(2)
+    pass_on(0)
+    phase(3)
+
+    def outputs(j, carry):
+        across_rows = (((0,), (0,)), ((), ()))
+        mixed = lax.dot_general(
+            vbuf[:, head(j)], pbuf[j], across_rows, preferred_element_type=jnp.float32
+        )
+        grad = scale * lax.dot_general(
+            kbuf[:, head(j)], wbuf[j], across_rows, preferred_element_type=jnp.float32
+        )
+        for r in range(REP):
+            cols = pl.ds(pl.multiple_of((j * REP + r) * DH, DH), DH)
+            att_ref[:, cols] = mixed[:, r * TOK : (r + 1) * TOK].T.astype(jnp.bfloat16)
+            gq_ref[:, cols] = grad[:, r * TOK : (r + 1) * TOK].T.astype(jnp.bfloat16)
+        return carry
+
+    lax.fori_loop(0, HK, outputs, 0)
+
+    pass_on(1)
+    pass_on(2)
+    last = ROWS - 1
+    for h, out in ((0, gk_ref), (1, gv_ref)):
+        cross(h, last).wait_recv()
+        acc[last, h] = acc[last, h] + xrecv[last, h].astype(jnp.float32)
+
+        @pl.when(z < ROWS - 1)
+        def _():
+            chain_in(h, z).wait_recv()
+            acc[last, h] = acc[last, h] + crecv[z, h].astype(jnp.float32)
+
+        @pl.when(z > 0)
+        def _():
+            chain_in(h, ROWS).wait_recv()
+            acc[last, h] = acc[last, h] + crecv[ROWS, h].astype(jnp.float32)
+
+        out[...] = acc[last, h].astype(jnp.bfloat16)
+
+    for h in (0, 1):
+        for zz in range(ROWS):
+            across(h, zz).wait_send()
+            cross(h, zz).wait_send()
+        for o in range(ROWS - 1):
+            chain(h, o).wait_send()
+        for k in range(1, ROWS):
+
+            @pl.when((z - (k - 1) >= 0) & (z < ROWS - 1))
+            def _():
+                along(h, k, True).wait_send()
+
+            @pl.when((z + (k - 1) < ROWS) & (z > 0))
+            def _():
+                along(h, k, False).wait_send()
+
+
+def dense(queries, keys, values, grad_out, positions):
+    tokens = TOK * 2 * ROWS
+    key_width = HK * DH
+    wide = REP * TOK
+    bf16, f32 = jnp.bfloat16, jnp.float32
+    vmem = pl.BlockSpec(memory_space=pltpu.VMEM)
+    dma = pltpu.SemaphoreType.DMA
+    return pl.pallas_call(
+        dense_kernel,
+        out_shape=[
+            jax.ShapeDtypeStruct((TOK, HQ * DH), bf16),
+            jax.ShapeDtypeStruct((TOK, HQ * DH), bf16),
+            jax.ShapeDtypeStruct((TOK, key_width), bf16),
+            jax.ShapeDtypeStruct((TOK, key_width), bf16),
+        ],
+        in_specs=[vmem] * 6,
+        out_specs=[vmem] * 4,
+        scratch_shapes=[
+            pltpu.VMEM((tokens, key_width), bf16),
+            pltpu.VMEM((tokens, key_width), bf16),
+            pltpu.VMEM((HK, DH, wide), bf16),
+            pltpu.VMEM((HK, DH, wide), bf16),
+            pltpu.VMEM((HK, wide, DH), bf16),
+            pltpu.VMEM((HK, wide, DH), bf16),
+            pltpu.VMEM((HK, tokens, wide), f32),
+            pltpu.VMEM((HK, tokens, wide), f32),
+            pltpu.VMEM((HK, tokens, wide), bf16),
+            pltpu.VMEM((HK, tokens, wide), bf16),
+            pltpu.VMEM((HK, 8, wide), f32),
+            pltpu.VMEM((HK, 8, wide), f32),
+            pltpu.VMEM((HK, 8, wide), f32),
+            pltpu.VMEM((ROWS, 2, TOK, key_width), f32),
+            pltpu.VMEM((ROWS, 2, TOK, key_width), bf16),
+            pltpu.VMEM((ROWS, 2, TOK, key_width), bf16),
+            pltpu.VMEM((ROWS - 1, 2, TOK, key_width), bf16),
+            pltpu.VMEM((ROWS + 1, 2, TOK, key_width), bf16),
+            dma((2, ROWS)),
+            dma((2, ROWS)),
+            dma((2, ROWS - 1)),
+            dma((2, ROWS - 1)),
+            dma((2, ROWS - 1)),
+            dma((2, ROWS - 1)),
+            dma((2, ROWS)),
+            dma((2, ROWS)),
+            dma((2, ROWS - 1)),
+            dma((2, ROWS + 1)),
+        ],
+        compiler_params=pltpu.CompilerParams(
+            collective_id=0, has_side_effects=True, vmem_limit_bytes=56 * 1024 * 1024
+        ),
+    )(
+        positions.reshape(1, -1), positions.reshape(-1, 1),
+        queries, keys, values, grad_out,
+    )
+
+
+def choose(queries, keys, values, grad_out, positions):
+    if lax.axis_size("ctx") == 2 * ROWS and queries.shape[0] == TOK:
+        return tuple(dense(queries, keys, values, grad_out, positions))
+    return local(queries, keys, values, grad_out, positions)
+
+
 def solution(mesh):
     in_specs = (
         P(("dp", "ctx"), None),
@@ -280,4 +670,4 @@
         P(("dp", "ctx"), None),
         P(("dp", "ctx"), None),
     )
-    return jax.shard_map(local, mesh=mesh, in_specs=in_specs, out_specs=out_specs, check_vma=False)
+    return jax.shard_map(choose, mesh=mesh, in_specs=in_specs, out_specs=out_specs, check_vma=False)

time: 455 us -> 65.3 us (0.14)
  waiting for transfers between devices: 219 us -> 0 us
  blocking collectives: 63.3 us -> 0 us
  local copies, waits for them, and re-layouts: 66.5 us -> 6.04 us
  Pallas kernels: 0 us -> 58.4 us
  other arithmetic: 53.4 us -> 0 us
  matrix products: 27.6 us -> 0 us
  between operations: 14.5 us -> 0.66 us
  starting transfers between devices: 9.09 us -> 0 us
    all_gather x2 -> x0, waiting for transfers between devices: 182 us -> none  [the longest x1 125 us: combined_all(): gathered = jax.tree.map(lambda a: lax.all_gather(a, axis), part)]
    all_gather x2 -> x0, blocking collectives: 63.3 us -> none  [combined_all(): gathered = jax.tree.map(lambda a: lax.all_gather(a, axis), part)]
    pallas_call x0 -> x1, Pallas kernels: none -> 58.4 us  [dense(): pl.pallas_call(dense_kernel, out_shape=[jax.ShapeDtypeStruct((TOK, HQ * D...]
    reduce_scatter x1 -> x0, waiting for transfers between devices: 29.2 us -> none  [local(): returned = lax.psum_scatter(laid, 'ctx', scatter_dimension=0, tiled=True)]
    dot_general x18 -> x0, matrix products: 27.6 us -> none  [the longest x1 3.23 us: local(): jnp.einsum('argu,uad->argd', weight_here, value_here.astype(jnp.float32),...]
    add x18 -> x0, other arithmetic: 25.6 us -> none  [the longest x7 18.8 us: combine_softmax(): left_summed * left_factor[..., None]]
    reshape x13 -> x1, local copies, waits for them, and re-layouts: 17.9 us -> 0.8 us  [dense(): positions.reshape(-1, 1)]
    gather x6 -> x0, local copies, waits for them, and re-layouts: 11.9 us -> none  [the longest x1 6.77 us: local(): compact = everyone[slot_of]]
  transfers between devices with their start and end apart: 7 -> 0, of which waited for: 5 -> 0; matrix products, arithmetic and copies ran while one was open for 16% -> 0% of each run, Pallas kernels for 0% -> 0%
where the time goes in v1:
time: 65.3 us; the launch traced here: 65.1 us
  Pallas kernels  58.4 us (89%)
  local copies, waits for them, and re-layouts  6.04 us (9%)
  between operations  0.66 us (1%)
    pallas_call x1, Pallas kernels, dense(): pl.pallas_call(dense_kernel, out_shape=[jax.ShapeDtypeStruct((TOK, HQ * D...  58.4 us
    unnamed x12, local copies, waits for them, and re-layouts  5.24 us

profile of v1, /device:TPU:0, one launch (start us, length us, event | category | flops | bytes accessed | tf_op | source)
XLA Modules:
  0.0 65.1 jit_solution(2629047060940769335)
XLA Ops:
  0.6 0.0 copy-start.3
  0.6 0.7 %copy-done.3 = s32[256]{0:T(256)S(1)} copy-done((s32[256]{0:T(256)S(1)}, s32[256]{0:T(256)}, u32[]{:S(2)}) %copy-start.3) | copy-done | bytes 1048
  1.3 0.8 %copy.9.pos_col = s32[256,1]{1,0:T(8,128)} copy(s32[256,1]{0,1:T(1,128)S(1)} %bitcast.3) | data formatting | bytes 2048 | tf_op jit(solution)/shard_map/reshape | solution.py:648
  2.1 58.4 %shard_map.84 = (bf16[128,2048]{1,0:T(8,128)(2,1)}, bf16[128,2048]{1,0:T(8,128)(2,1)}, bf16[128,512]{1,0:T(8,128)(2,1)}, bf16[128,512]{1,0:T(8,128)(2,1)}) custom-call(s32[1,256]{1,0:T(1,128)} %bitcast.2, s32[256,1]{1,0:T(8,128)} %copy.9.pos_col, bf16[128,2048]{1,0:T(8,128)(2,1)} %q_ref.1, bf16[128,512]{1,0:T(8,128)(2,1)} %k_ref.1, bf16[128,512]{1,0:T(8,128)(2,1)} %v_ref.1, ...), custom_call_target="tpu_custom_call" | custom-call | tf_op jit(solution)/shard_map/pallas_call | solution.py:604
  60.5 0.0 copy-start
  60.5 1.9 %copy.14 = bf16[128,2048]{1,0:T(8,128)(2,1)} copy(bf16[128,2048]{1,0:T(8,128)(2,1)} %get-tuple-element.8) | data formatting | bytes 1048576
  62.4 0.0 copy-done
  62.4 0.0 copy-start.2
  62.4 0.8 %copy.15 = bf16[128,2048]{1,0:T(8,128)(2,1)} copy(bf16[128,2048]{1,0:T(8,128)(2,1)S(1)} %copy-done) | data formatting | bytes 1048576
  63.2 0.2 copy-done.2
  63.5 0.0 copy-start.1
  63.5 0.7 %copy.16 = bf16[128,512]{1,0:T(8,128)(2,1)} copy(bf16[128,512]{1,0:T(8,128)(2,1)S(1)} %copy-done.2) | data formatting | bytes 262144
  64.1 0.3 copy-done.1
  64.4 0.7 %copy.17 = bf16[128,512]{1,0:T(8,128)(2,1)} copy(bf16[128,512]{1,0:T(8,128)(2,1)S(1)} %copy-done.1) | data formatting | bytes 262144
Async XLA Ops:
  0.6 0.7 %copy-start.3 = (s32[256]{0:T(256)S(1)}, s32[256]{0:T(256)}, u32[]{:S(2)}) copy-start(s32[256]{0:T(256)} %param.9) | copy-start | bytes 3076
  60.5 2.0 %copy-start = (bf16[128,2048]{1,0:T(8,128)(2,1)S(1)}, bf16[128,2048]{1,0:T(8,128)(2,1)}, u32[]{:S(2)}) copy-start(bf16[128,2048]{1,0:T(8,128)(2,1)} %get-tuple-element.9) | copy-start | bytes 1572868
  62.4 1.0 %copy-start.2 = (bf16[128,512]{1,0:T(8,128)(2,1)S(1)}, bf16[128,512]{1,0:T(8,128)(2,1)}, u32[]{:S(2)}) copy-start(bf16[128,512]{1,0:T(8,128)(2,1)} %get-tuple-element.10) | copy-start | bytes 393220
  63.5 1.0 %copy-start.1 = (bf16[128,512]{1,0:T(8,128)(2,1)S(1)}, bf16[128,512]{1,0:T(8,128)(2,1)}, u32[]{:S(2)}) copy-start(bf16[128,512]{1,0:T(8,128)(2,1)} %get-tuple-element.11) | copy-start | bytes 393220

commit v2 on v1

--- a/solution.py
+++ b/solution.py
@@ -277,17 +277,18 @@
 
 
 def dense_kernel(
-    pos_row, pos_col, q_ref, k_ref, v_ref, g_ref,
-    att_ref, gq_ref, gk_ref, gv_ref,
-    kbuf, vbuf, qt, gt, qs, gs, sbuf, dbuf, pbuf, wbuf, top8, inv, delta,
-    acc, xsend, xrecv, csend, crecv,
-    ax_s, ax_r, au_s, au_r, ad_s, ad_r, rx_s, rx_r, rc_s, rc_r,
+    pos_row, q_in, k_in, v_in, g_in,
+    att_out, gq_out, gk_ref, gv_ref,
+    q_ref, g_ref, att_ref, gq_ref,
+    kbuf, vbuf, qt, gt, qs, gs, sbuf, dbuf, pbuf, wbuf, top8, total8, mixed8,
+    acc, xsend, xrecv, csend, crecv, erecv,
+    in_s, out_s, ax_s, ax_r, au_s, au_r, ad_s, ad_r, ek_s, ek_r, rx_s, rx_r, rc_s, rc_r, ex_s, ex_r,
 ):
     c = lax.axis_index("ctx")
     z, x = c // 2, c % 2
     partner = c + 1 - 2 * x
     scale = 1.0 / math.sqrt(DH)
-    own = (k_ref, v_ref)
+    own = (k_in, v_in)
     bufs = (kbuf, vbuf)
     wide = REP * TOK
 
@@ -296,6 +297,15 @@
 
     def head(j):
         return pl.ds(pl.multiple_of(j * DH, DH), DH)
+
+    loads = [
+        pltpu.make_async_copy(source, target, in_s.at[i])
+        for i, (source, target) in enumerate(
+            ((k_in, kbuf.at[rows(c)]), (v_in, vbuf.at[rows(c)]), (q_in, q_ref), (g_in, g_ref))
+        )
+    ]
+    for load in loads:
+        load.start()
 
     barrier = pltpu.get_barrier_semaphore()
     pl.semaphore_signal(barrier, inc=1, device_id={"ctx": partner}, device_id_type=MESH)
@@ -354,8 +364,18 @@
         def _():
             along(h, 1, False, own[h]).start()
 
-    kbuf[rows(c), :] = k_ref[...]
-    vbuf[rows(c), :] = v_ref[...]
+    def beside(up):
+        here = kbuf.at[rows(2 * z + 1 - x)]
+        i = 0 if up else 1
+        return remote(here, here, ek_s.at[i], ek_r.at[i], c + 2 if up else c - 2)
+
+    def beside_in(up):
+        here = kbuf.at[rows(2 * (z - 1 if up else z + 1) + 1 - x)]
+        i = 0 if up else 1
+        return remote(here, here, ek_s.at[i], ek_r.at[i], partner)
+
+    for load in loads:
+        load.wait()
 
     def stack(j, carry):
         for r in range(REP):
@@ -370,18 +390,19 @@
 
     lax.fori_loop(0, HK, stack, 0)
     top8[...] = jnp.full(top8.shape, FAR, jnp.float32)
+    total8[...] = jnp.zeros(total8.shape, jnp.float32)
+    mixed8[...] = jnp.zeros(mixed8.shape, jnp.float32)
 
     glob_count = pos_row.shape[1]
-    row_token = c * TOK + lax.broadcasted_iota(jnp.int32, (glob_count, TOK), 1)
-    row_glob = jnp.max(
-        jnp.where(pos_col[...] == row_token, 1.0, 0.0), axis=0, keepdims=True
-    )
+
+    def is_glob(block):
+        token = block * TOK + lax.broadcasted_iota(jnp.int32, (TOK, glob_count), 0)
+        return jnp.max(jnp.where(pos_row[...] == token, 1.0, 0.0), axis=1, keepdims=True)
+
+    row_glob = jnp.broadcast_to(is_glob(c), (TOK, TOK)).T
 
     def block_bias(block):
-        col_token = block * TOK + lax.broadcasted_iota(jnp.int32, (TOK, glob_count), 0)
-        col_glob = jnp.max(
-            jnp.where(pos_row[...] == col_token, 1.0, 0.0), axis=1, keepdims=True
-        )
+        col_glob = is_glob(block)
         u_block = block * (TOK // BLOCK) + lax.broadcasted_iota(jnp.int32, (TOK, TOK), 0) // BLOCK
         t_block = c * (TOK // BLOCK) + lax.broadcasted_iota(jnp.int32, (TOK, TOK), 1) // BLOCK
         near = jnp.where(jnp.abs(u_block - t_block) <= 1, 1.0, 0.0)
@@ -393,19 +414,33 @@
         bias = block_bias(block)
         at = rows(block)
 
-        def one(j, carry):
-            s = jnp.dot(kbuf[at, head(j)], qt[j], preferred_element_type=jnp.float32)
+        for j in range(HK):
+            cols = slice(j * DH, (j + 1) * DH)
+            s = jnp.dot(kbuf[at, cols], qt[j], preferred_element_type=jnp.float32)
             s = s * scale + bias
             sbuf[j, at, :] = s
-            top8[j] = jnp.maximum(top8[j], jnp.max(s.reshape(TOK // 8, 8, wide), axis=0))
-            dbuf[j, at, :] = jnp.dot(
-                vbuf[at, head(j)], gt[j], preferred_element_type=jnp.float32
-            )
-            return carry
-
-        lax.fori_loop(0, HK, one, 0)
+            d = jnp.dot(vbuf[at, cols], gt[j], preferred_element_type=jnp.float32)
+            dbuf[j, at, :] = d
+            s = s.reshape(TOK // 8, 8, wide)
+            old = top8[j]
+            new = jnp.maximum(old, jnp.max(s, axis=0))
+            factor = jnp.exp(old - new)
+            e = jnp.exp(s - new[None])
+            top8[j] = new
+            total8[j] = total8[j] * factor + jnp.sum(e, axis=0)
+            e = e * d.reshape(TOK // 8, 8, wide)
+            mixed8[j] = mixed8[j] * factor + jnp.sum(e, axis=0)
 
     scores(c)
+    across_in(0, z).wait_recv()
+
+    @pl.when(z < ROWS - 1)
+    def _():
+        beside(True).start()
+
+    @pl.when(z > 0)
+    def _():
+        beside(False).start()
 
     def gather_step(k, carry):
         @pl.when(z - k >= 0)
@@ -417,7 +452,14 @@
                 def _():
                     along(h, k + 1, True).start()
 
-                across(h, z - k).start()
+                if h == 0:
+
+                    @pl.when(k > 1)
+                    def _():
+                        across(0, z - k).start()
+
+                else:
+                    across(1, z - k).start()
 
         @pl.when(z + k < ROWS)
         def _():
@@ -428,7 +470,14 @@
                 def _():
                     along(h, k + 1, False).start()
 
-                across(h, z + k).start()
+                if h == 0:
+
+                    @pl.when(k > 1)
+                    def _():
+                        across(0, z + k).start()
+
+                else:
+                    across(1, z + k).start()
 
         @pl.when(z - k >= 0)
         def _():
@@ -440,59 +489,57 @@
 
         @pl.when(z - (k - 1) >= 0)
         def _():
-            for h in (0, 1):
-                across_in(h, z - (k - 1)).wait_recv()
+            @pl.when(k == 2)
+            def _():
+                beside_in(True).wait_recv()
+
+            @pl.when(k > 2)
+            def _():
+                across_in(0, z - (k - 1)).wait_recv()
+
+            across_in(1, z - (k - 1)).wait_recv()
             scores(2 * (z - (k - 1)) + 1 - x)
 
         @pl.when((z + (k - 1) < ROWS) & (k > 1))
         def _():
-            for h in (0, 1):
-                across_in(h, z + (k - 1)).wait_recv()
+            @pl.when(k == 2)
+            def _():
+                beside_in(False).wait_recv()
+
+            @pl.when(k > 2)
+            def _():
+                across_in(0, z + (k - 1)).wait_recv()
+
+            across_in(1, z + (k - 1)).wait_recv()
             scores(2 * (z + (k - 1)) + 1 - x)
 
         return carry
 
     lax.fori_loop(1, ROWS + 1, gather_step, 0)
 
-    def stats(j, carry):
+    for j in range(HK):
         top = jnp.max(top8[j], axis=0, keepdims=True)
-
-        def part(b, sums):
-            total8, mixed8 = sums
-            at = rows(b)
-            e = jnp.exp(sbuf[j, at, :] - top)
-            sbuf[j, at, :] = e
-            total8 = total8 + jnp.sum(e.reshape(TOK // 8, 8, wide), axis=0)
-            e = e * dbuf[j, at, :]
-            return total8, mixed8 + jnp.sum(e.reshape(TOK // 8, 8, wide), axis=0)
-
-        zero = jnp.zeros((8, wide), jnp.float32)
-        total8, mixed8 = lax.fori_loop(0, 2 * ROWS, part, (zero, zero))
-        reciprocal = 1.0 / jnp.sum(total8, axis=0, keepdims=True)
-        inv[j] = jnp.broadcast_to(reciprocal, (8, wide))
-        delta[j] = jnp.broadcast_to(
-            jnp.sum(mixed8, axis=0, keepdims=True) * reciprocal, (8, wide)
-        )
-        return carry
-
-    lax.fori_loop(0, HK, stats, 0)
+        factor = jnp.exp(top8[j] - top)
+        reciprocal = 1.0 / jnp.sum(total8[j] * factor, axis=0, keepdims=True)
+        delta = jnp.sum(mixed8[j] * factor, axis=0, keepdims=True) * reciprocal
+        top8[j] = jnp.broadcast_to(top, (8, wide))
+        total8[j] = jnp.broadcast_to(reciprocal, (8, wide))
+        mixed8[j] = jnp.broadcast_to(delta, (8, wide))
 
     def terms(block, out):
         at = rows(block)
 
-        def one(j, carry):
-            p = sbuf[j, at, :] * inv[j, 0:1, :]
-            w = (p * (dbuf[j, at, :] - delta[j, 0:1, :])).astype(jnp.bfloat16)
+        for j in range(HK):
+            cols = slice(j * DH, (j + 1) * DH)
+            p = jnp.exp(sbuf[j, at, :] - top8[j, 0:1, :]) * total8[j, 0:1, :]
+            w = (p * (dbuf[j, at, :] - mixed8[j, 0:1, :])).astype(jnp.bfloat16)
             p = p.astype(jnp.bfloat16)
             pbuf[j, at, :] = p
             wbuf[j, at, :] = w
             dk = jnp.dot(w, qs[j], preferred_element_type=jnp.float32) * scale
             dv = jnp.dot(p, gs[j], preferred_element_type=jnp.float32)
-            out[0, :, head(j)] = dk.astype(out.dtype)
-            out[1, :, head(j)] = dv.astype(out.dtype)
-            return carry
-
-        lax.fori_loop(0, HK, one, 0)
+            out[0, :, cols] = dk.astype(out.dtype)
+            out[1, :, cols] = dv.astype(out.dtype)
 
     def pick(a, b, d, e):
         return jnp.where(z == 0, a, jnp.where(z == 1, b, jnp.where(z == 2, d, e)))
@@ -504,10 +551,50 @@
             xsend.at[o, h], xrecv.at[o, h], rx_s.at[h, o], rx_r.at[h, o], partner
         )
 
+    near = (None, (z == 1) | (z == 2), None, None)
+
+    def extra(o):
+        down = order[o] < z
+        i = jnp.where(down, 1, 0)
+        return remote(
+            xsend.at[o, 0], erecv.at[i], ex_s.at[i], ex_r.at[i], jnp.where(down, c - 2, c + 2)
+        )
+
+    def extra_in(i):
+        return remote(erecv.at[i], erecv.at[i], ex_s.at[i], ex_r.at[i], partner)
+
     def phase(o):
         terms(2 * order[o] + 1 - x, xsend.at[o])
-        for h in (0, 1):
-            cross(h, o).start()
+        if o == 2:
+            extra(2).start()
+        elif o == 1:
+
+            @pl.when(near[1])
+            def _():
+                extra(1).start()
+
+            @pl.when(jnp.logical_not(near[1]))
+            def _():
+                cross(0, 1).start()
+
+        elif o == 3:
+
+            @pl.when(z > 0)
+            def _():
+                extra_in(0).wait_recv()
+                both = xsend[3, 0].astype(jnp.float32) + erecv[0].astype(jnp.float32)
+                xsend[3, 0] = both.astype(jnp.bfloat16)
+
+            @pl.when(z < ROWS - 1)
+            def _():
+                extra_in(1).wait_recv()
+                both = xsend[3, 0].astype(jnp.float32) + erecv[1].astype(jnp.float32)
+                xsend[3, 0] = both.astype(jnp.bfloat16)
+
+            cross(0, 3).start()
+        else:
+            cross(0, 0).start()
+        cross(1, o).start()
         terms(2 * order[o] + x, acc.at[o])
 
     def chain(h, o):
@@ -521,25 +608,38 @@
     def chain_in(h, slot):
         return remote(crecv.at[slot, h], crecv.at[slot, h], rc_s.at[h, 0], rc_r.at[h, slot], partner)
 
-    def pass_on(o):
+    def pass_on(o, h):
         down = order[o] < z
         fed = (down & (z < ROWS - 1)) | (jnp.logical_not(down) & (z > 0))
-        for h in (0, 1):
+
+        def add_crossed():
             cross(h, o).wait_recv()
             acc[o, h] = acc[o, h] + xrecv[o, h].astype(jnp.float32)
 
-            @pl.when(fed)
-            def _():
-                chain_in(h, order[o]).wait_recv()
-                acc[o, h] = acc[o, h] + crecv[order[o], h].astype(jnp.float32)
-
-            csend[o, h] = acc[o, h].astype(jnp.bfloat16)
-            chain(h, o).start()
-
+        if h == 1 or o == 0:
+            add_crossed()
+        elif o == 1:
+            pl.when(jnp.logical_not(near[1]))(add_crossed)
+
+        @pl.when(fed)
+        def _():
+            chain_in(h, order[o]).wait_recv()
+            acc[o, h] = acc[o, h] + crecv[order[o], h].astype(jnp.float32)
+
+        csend[o, h] = acc[o, h].astype(jnp.bfloat16)
+        chain(h, o).start()
+
+    edge = (z == 0) | (z == ROWS - 1)
     phase(0)
     phase(1)
+    pass_on(0, 0)
     phase(2)
-    pass_on(0)
+
+    @pl.when(edge)
+    def _():
+        pass_on(2, 0)
+
+    pass_on(0, 1)
     phase(3)
 
     def outputs(j, carry):
@@ -556,10 +656,22 @@
             gq_ref[:, cols] = grad[:, r * TOK : (r + 1) * TOK].T.astype(jnp.bfloat16)
         return carry
 
-    lax.fori_loop(0, HK, outputs, 0)
-
-    pass_on(1)
-    pass_on(2)
+    lax.fori_loop(0, HK // 2, outputs, 0)
+    pass_on(1, 0)
+    lax.fori_loop(HK // 2, HK, outputs, 0)
+    stores = [
+        pltpu.make_async_copy(att_ref, att_out, out_s.at[0]),
+        pltpu.make_async_copy(gq_ref, gq_out, out_s.at[1]),
+    ]
+    for store in stores:
+        store.start()
+    pass_on(1, 1)
+
+    @pl.when(jnp.logical_not(edge))
+    def _():
+        pass_on(2, 0)
+
+    pass_on(2, 1)
     last = ROWS - 1
     for h, out in ((0, gk_ref), (1, gv_ref)):
         cross(h, last).wait_recv()
@@ -577,10 +689,40 @@
 
         out[...] = acc[last, h].astype(jnp.bfloat16)
 
+    for store in stores:
+        store.wait()
+    across(0, z).wait_send()
     for h in (0, 1):
-        for zz in range(ROWS):
-            across(h, zz).wait_send()
-            cross(h, zz).wait_send()
+        cross(h, 0).wait_send()
+        cross(h, 3).wait_send()
+    cross(1, 1).wait_send()
+    cross(1, 2).wait_send()
+    extra(2).wait_send()
+
+    @pl.when(near[1])
+    def _():
+        extra(1).wait_send()
+
+    @pl.when(jnp.logical_not(near[1]))
+    def _():
+        cross(0, 1).wait_send()
+
+    @pl.when(z < ROWS - 1)
+    def _():
+        beside(True).wait_send()
+
+    @pl.when(z > 0)
+    def _():
+        beside(False).wait_send()
+
+    for zz in range(ROWS):
+        across(1, zz).wait_send()
+
+        @pl.when(jnp.abs(z - zz) > 1)
+        def _():
+            across(0, zz).wait_send()
+
+    for h in (0, 1):
         for o in range(ROWS - 1):
             chain(h, o).wait_send()
         for k in range(1, ROWS):
@@ -592,6 +734,18 @@
             @pl.when((z + (k - 1) < ROWS) & (z > 0))
             def _():
                 along(h, k, False).wait_send()
+
+
+def copy_kernel(*refs):
+    sems = refs[-1]
+    count = len(refs) // 2
+    copies = [
+        pltpu.make_async_copy(refs[i], refs[count + i], sems.at[i]) for i in range(count)
+    ]
+    for copy in copies:
+        copy.start()
+    for copy in copies:
+        copy.wait()
 
 
 def dense(queries, keys, values, grad_out, positions):
@@ -601,17 +755,23 @@
     bf16, f32 = jnp.bfloat16, jnp.float32
     vmem = pl.BlockSpec(memory_space=pltpu.VMEM)
     dma = pltpu.SemaphoreType.DMA
-    return pl.pallas_call(
+    anywhere = pl.BlockSpec(memory_space=pl.ANY)
+    shapes = [
+        jax.ShapeDtypeStruct((TOK, HQ * DH), bf16),
+        jax.ShapeDtypeStruct((TOK, HQ * DH), bf16),
+        jax.ShapeDtypeStruct((TOK, key_width), bf16),
+        jax.ShapeDtypeStruct((TOK, key_width), bf16),
+    ]
+    results = pl.pallas_call(
         dense_kernel,
-        out_shape=[
-            jax.ShapeDtypeStruct((TOK, HQ * DH), bf16),
-            jax.ShapeDtypeStruct((TOK, HQ * DH), bf16),
-            jax.ShapeDtypeStruct((TOK, key_width), bf16),
-            jax.ShapeDtypeStruct((TOK, key_width), bf16),
-        ],
-        in_specs=[vmem] * 6,
-        out_specs=[vmem] * 4,
+        out_shape=shapes,
+        in_specs=[vmem] + [anywhere] * 4,
+        out_specs=[anywhere] * 2 + [vmem] * 2,
         scratch_shapes=[
+            pltpu.VMEM((TOK, HQ * DH), bf16),
+            pltpu.VMEM((TOK, HQ * DH), bf16),
+            pltpu.VMEM((TOK, HQ * DH), bf16),
+            pltpu.VMEM((TOK, HQ * DH), bf16),
             pltpu.VMEM((tokens, key_width), bf16),
             pltpu.VMEM((tokens, key_width), bf16),
             pltpu.VMEM((HK, DH, wide), bf16),
@@ -630,24 +790,35 @@
             pltpu.VMEM((ROWS, 2, TOK, key_width), bf16),
             pltpu.VMEM((ROWS - 1, 2, TOK, key_width), bf16),
             pltpu.VMEM((ROWS + 1, 2, TOK, key_width), bf16),
+            pltpu.VMEM((2, TOK, key_width), bf16),
+            dma((4,)),
+            dma((2,)),
             dma((2, ROWS)),
             dma((2, ROWS)),
             dma((2, ROWS - 1)),
             dma((2, ROWS - 1)),
             dma((2, ROWS - 1)),
             dma((2, ROWS - 1)),
+            dma((2,)),
+            dma((2,)),
             dma((2, ROWS)),
             dma((2, ROWS)),
             dma((2, ROWS - 1)),
             dma((2, ROWS + 1)),
+            dma((2,)),
+            dma((2,)),
         ],
         compiler_params=pltpu.CompilerParams(
             collective_id=0, has_side_effects=True, vmem_limit_bytes=56 * 1024 * 1024
         ),
-    )(
-        positions.reshape(1, -1), positions.reshape(-1, 1),
-        queries, keys, values, grad_out,
-    )
+    )(positions.reshape(1, -1), queries, keys, values, grad_out)
+    return pl.pallas_call(
+        copy_kernel,
+        out_shape=shapes,
+        in_specs=[anywhere] * 4,
+        out_specs=[anywhere] * 4,
+        scratch_shapes=[dma((4,))],
+    )(*results)
 
 
 def choose(queries, keys, values, grad_out, positions):

time: 65.3 us -> 102 us (1.56)
  Pallas kernels: 58.4 us -> 101 us
  local copies, waits for them, and re-layouts: 6.04 us -> 0 us
    pallas_call x1 -> x2, Pallas kernels: 58.4 us -> 101 us  [the longest x1 60.4 us: dense(): pl.pallas_call(dense_kernel, out_shape=shapes, in_specs=[vmem] + [anywher...]
    unnamed x12 -> x0, local copies, waits for them, and re-layouts: 5.24 us -> none
where the time goes in v2:
time: 102 us
  Pallas kernels  101 us (99%)
    pallas_call x1, Pallas kernels, dense(): pl.pallas_call(dense_kernel, out_shape=shapes, in_specs=[vmem] + [anywher...  60.4 us
    pallas_call x1, Pallas kernels, dense(): pl.pallas_call(copy_kernel, out_shape=shapes, in_specs=[anywhere] * 4, ou...  40.8 us

profile of v2, /device:TPU:0, one launch (start us, length us, event | category | flops | bytes accessed | tf_op | source)
XLA Modules:
  0.0 101.8 jit_solution(4255266580611365630)
XLA Ops:
  0.6 60.4 %shard_map.84 = (bf16[128,2048]{1,0:T(8,128)(2,1)}, bf16[128,2048]{1,0:T(8,128)(2,1)}, bf16[128,512]{1,0:T(8,128)(2,1)}, bf16[128,512]{1,0:T(8,128)(2,1)}) custom-call(s32[1,256]{1,0:T(1,128)} %bitcast.1, bf16[128,2048]{1,0:T(8,128)(2,1)} %q_in.1, bf16[128,512]{1,0:T(8,128)(2,1)} %k_in.1, bf16[128,512]{1,0:T(8,128)(2,1)} %v_in.1, bf16[128,2048]{1,0:T(8,128)(2,1)} %g_in.1), custom_call_target="tpu_custom_call" | custom-call | tf_op jit(solution)/shard_map/pallas_call | solution.py:765
  61.0 40.8 %shard_map.85 = (bf16[128,2048]{1,0:T(8,128)(2,1)}, bf16[128,2048]{1,0:T(8,128)(2,1)}, bf16[128,512]{1,0:T(8,128)(2,1)}, bf16[128,512]{1,0:T(8,128)(2,1)}) custom-call(bf16[128,2048]{1,0:T(8,128)(2,1)} %get-tuple-element.8.refs_0_, bf16[128,2048]{1,0:T(8,128)(2,1)} %get-tuple-element.9.refs_1_, bf16[128,512]{1,0:T(8,128)(2,1)} %get-tuple-element.10.refs_2_, ...), custom_call_target="tpu_custom_call" | custom-call | tf_op jit(solution)/shard_map/pallas_call | solution.py:815

commit v3 on v2

--- a/solution.py
+++ b/solution.py
@@ -280,7 +280,7 @@
     pos_row, q_in, k_in, v_in, g_in,
     att_out, gq_out, gk_ref, gv_ref,
     q_ref, g_ref, att_ref, gq_ref,
-    kbuf, vbuf, qt, gt, qs, gs, sbuf, dbuf, pbuf, wbuf, top8, total8, mixed8,
+    kv, qt, gt, qs, gs, sbuf, dbuf, pbuf, wbuf, top8, total8, mixed8,
     acc, xsend, xrecv, csend, crecv, erecv,
     in_s, out_s, ax_s, ax_r, au_s, au_r, ad_s, ad_r, ek_s, ek_r, rx_s, rx_r, rc_s, rc_r, ex_s, ex_r,
 ):
@@ -288,8 +288,7 @@
     z, x = c // 2, c % 2
     partner = c + 1 - 2 * x
     scale = 1.0 / math.sqrt(DH)
-    own = (k_in, v_in)
-    bufs = (kbuf, vbuf)
+    half = HK // 2 * DH
     wide = REP * TOK
 
     def rows(block):
@@ -301,7 +300,12 @@
     loads = [
         pltpu.make_async_copy(source, target, in_s.at[i])
         for i, (source, target) in enumerate(
-            ((k_in, kbuf.at[rows(c)]), (v_in, vbuf.at[rows(c)]), (q_in, q_ref), (g_in, g_ref))
+            [
+                (source.at[:, pl.ds(h * half, half)], kv.at[h, rows(c), pl.ds(i * half, half)])
+                for h in (0, 1)
+                for i, source in enumerate((k_in, v_in))
+            ]
+            + [(q_in, q_ref), (g_in, g_ref)]
         )
     ]
     for load in loads:
@@ -328,53 +332,55 @@
             device_id={"ctx": device}, device_id_type=MESH,
         )
 
-    def along(h, k, up, source=None):
+    def along(h, k, up):
         block = c - 2 * (k - 1) if up else c + 2 * (k - 1)
-        here = bufs[h].at[rows(block)]
+        here = kv.at[h, rows(block)]
         send, recv = (au_s, au_r) if up else (ad_s, ad_r)
         return remote(
-            here if source is None else source, here,
+            here, here,
             send.at[h, k - 1], recv.at[h, k - 1], c + 2 if up else c - 2,
         )
 
     def along_in(h, k, up):
         block = c - 2 * k if up else c + 2 * k
-        here = bufs[h].at[rows(block)]
+        here = kv.at[h, rows(block)]
         send, recv = (au_s, au_r) if up else (ad_s, ad_r)
         return remote(here, here, send.at[h, k - 1], recv.at[h, k - 1], partner)
 
-    def across(h, zz, source=None):
-        here = bufs[h].at[rows(2 * zz + x)]
-        return remote(
-            here if source is None else source, here, ax_s.at[h, zz], ax_r.at[h, zz], partner
-        )
+    def across(h, zz):
+        here = kv.at[h, rows(2 * zz + x)]
+        return remote(here, here, ax_s.at[h, zz], ax_r.at[h, zz], partner)
 
     def across_in(h, zz):
-        here = bufs[h].at[rows(2 * zz + 1 - x)]
+        here = kv.at[h, rows(2 * zz + 1 - x)]
         return remote(here, here, ax_s.at[h, zz], ax_r.at[h, zz], partner)
 
-    for h in (0, 1):
-        across(h, z, own[h]).start()
+    def send_own(h):
+        loads[2 * h].wait()
+        loads[2 * h + 1].wait()
+        across(h, z).start()
 
         @pl.when(z < ROWS - 1)
         def _():
-            along(h, 1, True, own[h]).start()
+            along(h, 1, True).start()
 
         @pl.when(z > 0)
         def _():
-            along(h, 1, False, own[h]).start()
+            along(h, 1, False).start()
+
+    send_own(0)
 
     def beside(up):
-        here = kbuf.at[rows(2 * z + 1 - x)]
+        here = kv.at[0, rows(2 * z + 1 - x)]
         i = 0 if up else 1
         return remote(here, here, ek_s.at[i], ek_r.at[i], c + 2 if up else c - 2)
 
     def beside_in(up):
-        here = kbuf.at[rows(2 * (z - 1 if up else z + 1) + 1 - x)]
+        here = kv.at[0, rows(2 * (z - 1 if up else z + 1) + 1 - x)]
         i = 0 if up else 1
         return remote(here, here, ek_s.at[i], ek_r.at[i], partner)
 
-    for load in loads:
+    for load in loads[4:]:
         load.wait()
 
     def stack(j, carry):
@@ -410,16 +416,18 @@
         bias = jnp.where(allowed > 0.5, 0.0, FAR)
         return jnp.concatenate([bias] * REP, axis=1)
 
-    def scores(block):
+    def scores(h, block):
         bias = block_bias(block)
         at = rows(block)
 
-        for j in range(HK):
-            cols = slice(j * DH, (j + 1) * DH)
-            s = jnp.dot(kbuf[at, cols], qt[j], preferred_element_type=jnp.float32)
+        def one(i, carry):
+            j = 2 * h + i
+            s = jnp.dot(kv[h, at, head(i)], qt[j], preferred_element_type=jnp.float32)
             s = s * scale + bias
             sbuf[j, at, :] = s
-            d = jnp.dot(vbuf[at, cols], gt[j], preferred_element_type=jnp.float32)
+            d = jnp.dot(
+                kv[h, at, head(i + HK // 2)], gt[j], preferred_element_type=jnp.float32
+            )
             dbuf[j, at, :] = d
             s = s.reshape(TOK // 8, 8, wide)
             old = top8[j]
@@ -430,107 +438,81 @@
             total8[j] = total8[j] * factor + jnp.sum(e, axis=0)
             e = e * d.reshape(TOK // 8, 8, wide)
             mixed8[j] = mixed8[j] * factor + jnp.sum(e, axis=0)
-
-    scores(c)
-    across_in(0, z).wait_recv()
-
-    @pl.when(z < ROWS - 1)
-    def _():
-        beside(True).start()
-
-    @pl.when(z > 0)
-    def _():
-        beside(False).start()
-
-    def gather_step(k, carry):
+            return carry
+
+        lax.fori_loop(0, HK // 2, one, 0)
+
+    edge = (z == 0) | (z == ROWS - 1)
+    two = jnp.where(z >= 2, z - 2, z + 2)
+
+    def forward(h, k):
         @pl.when(z - k >= 0)
         def _():
-            for h in (0, 1):
-                along_in(h, k, True).wait_recv()
+            along_in(h, k, True).wait_recv()
+
+            if k < ROWS - 1:
 
                 @pl.when(z < ROWS - 1)
                 def _():
                     along(h, k + 1, True).start()
 
-                if h == 0:
-
-                    @pl.when(k > 1)
-                    def _():
-                        across(0, z - k).start()
-
-                else:
-                    across(1, z - k).start()
+            if h == 1 or k > 1:
+                across(h, z - k).start()
 
         @pl.when(z + k < ROWS)
         def _():
-            for h in (0, 1):
-                along_in(h, k, False).wait_recv()
+            along_in(h, k, False).wait_recv()
+
+            if k < ROWS - 1:
 
                 @pl.when(z > 0)
                 def _():
                     along(h, k + 1, False).start()
 
-                if h == 0:
-
-                    @pl.when(k > 1)
-                    def _():
-                        across(0, z + k).start()
-
-                else:
-                    across(1, z + k).start()
-
-        @pl.when(z - k >= 0)
-        def _():
-            scores(c - 2 * k)
-
-        @pl.when(z + k < ROWS)
-        def _():
-            scores(c + 2 * k)
-
-        @pl.when(z - (k - 1) >= 0)
-        def _():
-            @pl.when(k == 2)
-            def _():
-                beside_in(True).wait_recv()
-
-            @pl.when(k > 2)
-            def _():
-                across_in(0, z - (k - 1)).wait_recv()
-
-            across_in(1, z - (k - 1)).wait_recv()
-            scores(2 * (z - (k - 1)) + 1 - x)
-
-        @pl.when((z + (k - 1) < ROWS) & (k > 1))
-        def _():
-            @pl.when(k == 2)
-            def _():
-                beside_in(False).wait_recv()
-
-            @pl.when(k > 2)
-            def _():
-                across_in(0, z + (k - 1)).wait_recv()
-
-            across_in(1, z + (k - 1)).wait_recv()
-            scores(2 * (z + (k - 1)) + 1 - x)
-
-        return carry
-
-    lax.fori_loop(1, ROWS + 1, gather_step, 0)
-
-    for j in range(HK):
-        top = jnp.max(top8[j], axis=0, keepdims=True)
-        factor = jnp.exp(top8[j] - top)
-        reciprocal = 1.0 / jnp.sum(total8[j] * factor, axis=0, keepdims=True)
-        delta = jnp.sum(mixed8[j] * factor, axis=0, keepdims=True) * reciprocal
-        top8[j] = jnp.broadcast_to(top, (8, wide))
-        total8[j] = jnp.broadcast_to(reciprocal, (8, wide))
-        mixed8[j] = jnp.broadcast_to(delta, (8, wide))
-
-    def terms(block, out):
+            if h == 1 or k > 1:
+                across(h, z + k).start()
+
+    def scores_next(h, other):
+        @pl.when(z > 0)
+        def _():
+            if other:
+                (beside_in(True) if h == 0 else across_in(1, z - 1)).wait_recv()
+            scores(h, 2 * (z - 1) + (1 - x if other else x))
+
+        @pl.when(z < ROWS - 1)
+        def _():
+            if other:
+                (beside_in(False) if h == 0 else across_in(1, z + 1)).wait_recv()
+            scores(h, 2 * (z + 1) + (1 - x if other else x))
+
+    def scores_far(h, k, other):
+        zz = two if k == 2 else ROWS - 1 - z
+
+        def go():
+            if other:
+                across_in(h, zz).wait_recv()
+            scores(h, 2 * zz + (1 - x if other else x))
+
+        if k == 2:
+            go()
+        else:
+            pl.when(edge)(go)
+
+    def stats(h):
+        for j in (2 * h, 2 * h + 1):
+            top = jnp.max(top8[j], axis=0, keepdims=True)
+            factor = jnp.exp(top8[j] - top)
+            reciprocal = 1.0 / jnp.sum(total8[j] * factor, axis=0, keepdims=True)
+            delta = jnp.sum(mixed8[j] * factor, axis=0, keepdims=True) * reciprocal
+            top8[j] = jnp.broadcast_to(top, (8, wide))
+            total8[j] = jnp.broadcast_to(reciprocal, (8, wide))
+            mixed8[j] = jnp.broadcast_to(delta, (8, wide))
+
+    def terms(h, block, out):
         at = rows(block)
 
-        for j in range(HK):
-            cols = slice(j * DH, (j + 1) * DH)
+        def one(i, carry):
+            j = 2 * h + i
             p = jnp.exp(sbuf[j, at, :] - top8[j, 0:1, :]) * total8[j, 0:1, :]
             w = (p * (dbuf[j, at, :] - mixed8[j, 0:1, :])).astype(jnp.bfloat16)
             p = p.astype(jnp.bfloat16)
@@ -538,8 +520,11 @@
             wbuf[j, at, :] = w
             dk = jnp.dot(w, qs[j], preferred_element_type=jnp.float32) * scale
             dv = jnp.dot(p, gs[j], preferred_element_type=jnp.float32)
-            out[0, :, cols] = dk.astype(out.dtype)
-            out[1, :, cols] = dv.astype(out.dtype)
+            out[:, head(i)] = dk.astype(out.dtype)
+            out[:, head(i + HK // 2)] = dv.astype(out.dtype)
+            return carry
+
+        lax.fori_loop(0, HK // 2, one, 0)
 
     def pick(a, b, d, e):
         return jnp.where(z == 0, a, jnp.where(z == 1, b, jnp.where(z == 2, d, e)))
@@ -563,9 +548,11 @@
     def extra_in(i):
         return remote(erecv.at[i], erecv.at[i], ex_s.at[i], ex_r.at[i], partner)
 
-    def phase(o):
-        terms(2 * order[o] + 1 - x, xsend.at[o])
-        if o == 2:
+    def phase(h, o):
+        terms(h, 2 * order[o] + 1 - x, xsend.at[o, h])
+        if h == 1 or o == 0:
+            cross(h, o).start()
+        elif o == 2:
             extra(2).start()
         elif o == 1:
 
@@ -577,7 +564,7 @@
             def _():
                 cross(0, 1).start()
 
-        elif o == 3:
+        else:
 
             @pl.when(z > 0)
             def _():
@@ -592,10 +579,7 @@
                 xsend[3, 0] = both.astype(jnp.bfloat16)
 
             cross(0, 3).start()
-        else:
-            cross(0, 0).start()
-        cross(1, o).start()
-        terms(2 * order[o] + x, acc.at[o])
+        terms(h, 2 * order[o] + x, acc.at[o, h])
 
     def chain(h, o):
         down = order[o] < z
@@ -608,7 +592,7 @@
     def chain_in(h, slot):
         return remote(crecv.at[slot, h], crecv.at[slot, h], rc_s.at[h, 0], rc_r.at[h, slot], partner)
 
-    def pass_on(o, h):
+    def pass_on(h, o):
         down = order[o] < z
         fed = (down & (z < ROWS - 1)) | (jnp.logical_not(down) & (z > 0))
 
@@ -629,65 +613,112 @@
         csend[o, h] = acc[o, h].astype(jnp.bfloat16)
         chain(h, o).start()
 
-    edge = (z == 0) | (z == ROWS - 1)
-    phase(0)
-    phase(1)
+    def outputs(h):
+        def one(i, carry):
+            j = 2 * h + i
+            over_keys = (((0,), (0,)), ((), ()))
+            mixed = lax.dot_general(
+                kv[h, :, head(i + HK // 2)], pbuf[j], over_keys,
+                preferred_element_type=jnp.float32,
+            )
+            grad = scale * lax.dot_general(
+                kv[h, :, head(i)], wbuf[j], over_keys, preferred_element_type=jnp.float32
+            )
+            for r in range(REP):
+                cols = pl.ds(pl.multiple_of((j * REP + r) * DH, DH), DH)
+                att_ref[:, cols] = mixed[:, r * TOK : (r + 1) * TOK].T.astype(jnp.bfloat16)
+                gq_ref[:, cols] = grad[:, r * TOK : (r + 1) * TOK].T.astype(jnp.bfloat16)
+            return carry
+
+        lax.fori_loop(0, HK // 2, one, 0)
+
+    def finish(h):
+        last = ROWS - 1
+        cross(h, last).wait_recv()
+        acc[last, h] = acc[last, h] + xrecv[last, h].astype(jnp.float32)
+
+        @pl.when(z < ROWS - 1)
+        def _():
+            chain_in(h, z).wait_recv()
+            acc[last, h] = acc[last, h] + crecv[z, h].astype(jnp.float32)
+
+        @pl.when(z > 0)
+        def _():
+            chain_in(h, ROWS).wait_recv()
+            acc[last, h] = acc[last, h] + crecv[ROWS, h].astype(jnp.float32)
+
+        gk_ref[:, h * half : (h + 1) * half] = acc[last, h, :, :half].astype(jnp.bfloat16)
+        gv_ref[:, h * half : (h + 1) * half] = acc[last, h, :, half:].astype(jnp.bfloat16)
+
+    scores(0, c)
+    forward(0, 1)
+    send_own(1)
+    across_in(0, z).wait_recv()
+
+    @pl.when(z < ROWS - 1)
+    def _():
+        beside(True).start()
+
+    @pl.when(z > 0)
+    def _():
+        beside(False).start()
+
+    scores_next(0, False)
+    forward(0, 2)
+    scores(0, 2 * z + 1 - x)
+    forward(1, 1)
+    scores_far(0, 2, False)
+    forward(0, 3)
+    scores_next(0, True)
+    forward(1, 2)
+    scores_far(0, 3, False)
+    scores_far(0, 2, True)
+    scores_far(0, 3, True)
+    stats(0)
+    phase(0, 0)
+    forward(1, 3)
+    scores(1, c)
+    across_in(1, z).wait_recv()
+    scores(1, 2 * z + 1 - x)
+    phase(0, 1)
+    scores_next(1, False)
+    phase(0, 2)
+
+    @pl.when(edge)
+    def _():
+        pass_on(0, 2)
+
     pass_on(0, 0)
-    phase(2)
-
-    @pl.when(edge)
-    def _():
-        pass_on(2, 0)
-
+    scores_far(1, 2, False)
+    scores_next(1, True)
+    phase(0, 3)
+    scores_far(1, 3, False)
+    scores_far(1, 2, True)
+    scores_far(1, 3, True)
+    stats(1)
+    phase(1, 0)
     pass_on(0, 1)
-    phase(3)
-
-    def outputs(j, carry):
-        across_rows = (((0,), (0,)), ((), ()))
-        mixed = lax.dot_general(
-            vbuf[:, head(j)], pbuf[j], across_rows, preferred_element_type=jnp.float32
-        )
-        grad = scale * lax.dot_general(
-            kbuf[:, head(j)], wbuf[j], across_rows, preferred_element_type=jnp.float32
-        )
-        for r in range(REP):
-            cols = pl.ds(pl.multiple_of((j * REP + r) * DH, DH), DH)
-            att_ref[:, cols] = mixed[:, r * TOK : (r + 1) * TOK].T.astype(jnp.bfloat16)
-            gq_ref[:, cols] = grad[:, r * TOK : (r + 1) * TOK].T.astype(jnp.bfloat16)
-        return carry
-
-    lax.fori_loop(0, HK // 2, outputs, 0)
+    phase(1, 1)
+
+    @pl.when(jnp.logical_not(edge))
+    def _():
+        pass_on(0, 2)
+
+    phase(1, 2)
     pass_on(1, 0)
-    lax.fori_loop(HK // 2, HK, outputs, 0)
+    phase(1, 3)
+    finish(0)
+    outputs(0)
+    pass_on(1, 1)
+    outputs(1)
     stores = [
         pltpu.make_async_copy(att_ref, att_out, out_s.at[0]),
         pltpu.make_async_copy(gq_ref, gq_out, out_s.at[1]),
     ]
     for store in stores:
         store.start()
-    pass_on(1, 1)
-
-    @pl.when(jnp.logical_not(edge))
-    def _():
-        pass_on(2, 0)
-
-    pass_on(2, 1)
-    last = ROWS - 1
-    for h, out in ((0, gk_ref), (1, gv_ref)):
-        cross(h, last).wait_recv()
-        acc[last, h] = acc[last, h] + xrecv[last, h].astype(jnp.float32)
-
-        @pl.when(z < ROWS - 1)
-        def _():
-            chain_in(h, z).wait_recv()
-            acc[last, h] = acc[last, h] + crecv[z, h].astype(jnp.float32)
-
-        @pl.when(z > 0)
-        def _():
-            chain_in(h, ROWS).wait_recv()
-            acc[last, h] = acc[last, h] + crecv[ROWS, h].astype(jnp.float32)
-
-        out[...] = acc[last, h].astype(jnp.bfloat16)
+    pass_on(1, 2)
+    finish(1)
 
     for store in stores:
         store.wait()
@@ -737,15 +768,18 @@
 
 
 def copy_kernel(*refs):
-    sems = refs[-1]
-    count = len(refs) // 2
-    copies = [
-        pltpu.make_async_copy(refs[i], refs[count + i], sems.at[i]) for i in range(count)
-    ]
-    for copy in copies:
-        copy.start()
-    for copy in copies:
-        copy.wait()
+    count = 4
+    ins, outs, held = (refs[i * count : (i + 1) * count] for i in range(3))
+    sems = refs[3 * count]
+    loads = [pltpu.make_async_copy(ins[i], held[i], sems.at[0, i]) for i in range(count)]
+    stores = [pltpu.make_async_copy(held[i], outs[i], sems.at[1, i]) for i in range(count)]
+    for load in loads:
+        load.start()
+    for load, store in zip(loads, stores):
+        load.wait()
+        store.start()
+    for store in stores:
+        store.wait()
 
 
 def dense(queries, keys, values, grad_out, positions):
@@ -772,8 +806,7 @@
             pltpu.VMEM((TOK, HQ * DH), bf16),
             pltpu.VMEM((TOK, HQ * DH), bf16),
             pltpu.VMEM((TOK, HQ * DH), bf16),
-            pltpu.VMEM((tokens, key_width), bf16),
-            pltpu.VMEM((tokens, key_width), bf16),
+            pltpu.VMEM((2, tokens, key_width), bf16),
             pltpu.VMEM((HK, DH, wide), bf16),
             pltpu.VMEM((HK, DH, wide), bf16),
             pltpu.VMEM((HK, wide, DH), bf16),
@@ -791,7 +824,7 @@
             pltpu.VMEM((ROWS - 1, 2, TOK, key_width), bf16),
             pltpu.VMEM((ROWS + 1, 2, TOK, key_width), bf16),
             pltpu.VMEM((2, TOK, key_width), bf16),
-            dma((4,)),
+            dma((6,)),
             dma((2,)),
             dma((2, ROWS)),
             dma((2, ROWS)),
@@ -817,7 +850,7 @@
         out_shape=shapes,
         in_specs=[anywhere] * 4,
         out_specs=[anywhere] * 4,
-        scratch_shapes=[dma((4,))],
+        scratch_shapes=[pltpu.VMEM(a.shape, bf16) for a in shapes] + [dma((2, 4))],
     )(*results)
 
 

time: 102 us -> 63 us (0.62)
  Pallas kernels: 101 us -> 62.2 us
    pallas_call x1, Pallas kernels: 40.8 us -> 2.16 us  [dense(): pl.pallas_call(copy_kernel, out_shape=shapes, in_specs=[anywhere] * 4, ou...]
where the time goes in v3:
time: 63 us; the launch traced here: 62.8 us
  Pallas kernels  62.2 us (99%)
  between operations  0.64 us (1%)
    pallas_call x1, Pallas kernels, dense(): pl.pallas_call(dense_kernel, out_shape=shapes, in_specs=[vmem] + [anywher...  60 us
    pallas_call x1, Pallas kernels, dense(): pl.pallas_call(copy_kernel, out_shape=shapes, in_specs=[anywhere] * 4, ou...  2.16 us

profile of v3, /device:TPU:0, one launch (start us, length us, event | category | flops | bytes accessed | tf_op | source)
XLA Modules:
  0.0 62.8 jit_solution(104951939887925941)
XLA Ops:
  0.6 60.0 %shard_map.84 = (bf16[128,2048]{1,0:T(8,128)(2,1)}, bf16[128,2048]{1,0:T(8,128)(2,1)}, bf16[128,512]{1,0:T(8,128)(2,1)}, bf16[128,512]{1,0:T(8,128)(2,1)}) custom-call(s32[1,256]{1,0:T(1,128)} %bitcast.1, bf16[128,2048]{1,0:T(8,128)(2,1)} %q_in.1, bf16[128,512]{1,0:T(8,128)(2,1)} %k_in.1, bf16[128,512]{1,0:T(8,128)(2,1)} %v_in.1, bf16[128,2048]{1,0:T(8,128)(2,1)} %g_in.1), custom_call_target="tpu_custom_call" | custom-call | tf_op jit(solution)/shard_map/pallas_call | solution.py:799
  60.6 2.2 %shard_map.85 = (bf16[128,2048]{1,0:T(8,128)(2,1)}, bf16[128,2048]{1,0:T(8,128)(2,1)}, bf16[128,512]{1,0:T(8,128)(2,1)}, bf16[128,512]{1,0:T(8,128)(2,1)}) custom-call(bf16[128,2048]{1,0:T(8,128)(2,1)} %get-tuple-element.8.refs_0_, bf16[128,2048]{1,0:T(8,128)(2,1)} %get-tuple-element.9.refs_1_, bf16[128,512]{1,0:T(8,128)(2,1)} %get-tuple-element.10.refs_2_, ...), custom_call_target="tpu_custom_call" | custom-call | tf_op jit(solution)/shard_map/pallas_call | solution.py:848

commit v4 on v2

--- a/solution.py
+++ b/solution.py
@@ -281,8 +281,8 @@
     att_out, gq_out, gk_ref, gv_ref,
     q_ref, g_ref, att_ref, gq_ref,
     kbuf, vbuf, qt, gt, qs, gs, sbuf, dbuf, pbuf, wbuf, top8, total8, mixed8,
-    acc, xsend, xrecv, csend, crecv, erecv,
-    in_s, out_s, ax_s, ax_r, au_s, au_r, ad_s, ad_r, ek_s, ek_r, rx_s, rx_r, rc_s, rc_r, ex_s, ex_r,
+    acc, xsend, xrecv, csend, crecv,
+    in_s, out_s, ax_s, ax_r, au_s, au_r, ad_s, ad_r, rx_s, rx_r, rc_s, rc_r,
 ):
     c = lax.axis_index("ctx")
     z, x = c // 2, c % 2
@@ -363,16 +363,6 @@
         @pl.when(z > 0)
         def _():
             along(h, 1, False, own[h]).start()
-
-    def beside(up):
-        here = kbuf.at[rows(2 * z + 1 - x)]
-        i = 0 if up else 1
-        return remote(here, here, ek_s.at[i], ek_r.at[i], c + 2 if up else c - 2)
-
-    def beside_in(up):
-        here = kbuf.at[rows(2 * (z - 1 if up else z + 1) + 1 - x)]
-        i = 0 if up else 1
-        return remote(here, here, ek_s.at[i], ek_r.at[i], partner)
 
     for load in loads:
         load.wait()
@@ -414,8 +404,8 @@
         bias = block_bias(block)
         at = rows(block)
 
-        for j in range(HK):
-            cols = slice(j * DH, (j + 1) * DH)
+        def one(j, carry):
+            cols = head(j)
             s = jnp.dot(kbuf[at, cols], qt[j], preferred_element_type=jnp.float32)
             s = s * scale + bias
             sbuf[j, at, :] = s
@@ -430,18 +420,11 @@
             total8[j] = total8[j] * factor + jnp.sum(e, axis=0)
             e = e * d.reshape(TOK // 8, 8, wide)
             mixed8[j] = mixed8[j] * factor + jnp.sum(e, axis=0)
+            return carry
+
+        lax.fori_loop(0, HK, one, 0)
 
     scores(c)
-    across_in(0, z).wait_recv()
-
-    @pl.when(z < ROWS - 1)
-    def _():
-        beside(True).start()
-
-    @pl.when(z > 0)
-    def _():
-        beside(False).start()
-
     def gather_step(k, carry):
         @pl.when(z - k >= 0)
         def _():
@@ -452,14 +435,7 @@
                 def _():
                     along(h, k + 1, True).start()
 
-                if h == 0:
-
-                    @pl.when(k > 1)
-                    def _():
-                        across(0, z - k).start()
-
-                else:
-                    across(1, z - k).start()
+                across(h, z - k).start()
 
         @pl.when(z + k < ROWS)
         def _():
@@ -470,14 +446,7 @@
                 def _():
                     along(h, k + 1, False).start()
 
-                if h == 0:
-
-                    @pl.when(k > 1)
-                    def _():
-                        across(0, z + k).start()
-
-                else:
-                    across(1, z + k).start()
+                across(h, z + k).start()
 
         @pl.when(z - k >= 0)
         def _():
@@ -489,28 +458,14 @@
 
         @pl.when(z - (k - 1) >= 0)
         def _():
-            @pl.when(k == 2)
-            def _():
-                beside_in(True).wait_recv()
-
-            @pl.when(k > 2)
-            def _():
-                across_in(0, z - (k - 1)).wait_recv()
-
-            across_in(1, z - (k - 1)).wait_recv()
+            for h in (0, 1):
+                across_in(h, z - (k - 1)).wait_recv()
             scores(2 * (z - (k - 1)) + 1 - x)
 
         @pl.when((z + (k - 1) < ROWS) & (k > 1))
         def _():
-            @pl.when(k == 2)
-            def _():
-                beside_in(False).wait_recv()
-
-            @pl.when(k > 2)
-            def _():
-                across_in(0, z + (k - 1)).wait_recv()
-
-            across_in(1, z + (k - 1)).wait_recv()
+            for h in (0, 1):
+                across_in(h, z + (k - 1)).wait_recv()
             scores(2 * (z + (k - 1)) + 1 - x)
 
         return carry
@@ -529,8 +484,8 @@
     def terms(block, out):
         at = rows(block)
 
-        for j in range(HK):
-            cols = slice(j * DH, (j + 1) * DH)
+        def one(j, carry):
+            cols = head(j)
             p = jnp.exp(sbuf[j, at, :] - top8[j, 0:1, :]) * total8[j, 0:1, :]
             w = (p * (dbuf[j, at, :] - mixed8[j, 0:1, :])).astype(jnp.bfloat16)
             p = p.astype(jnp.bfloat16)
@@ -540,6 +495,9 @@
             dv = jnp.dot(p, gs[j], preferred_element_type=jnp.float32)
             out[0, :, cols] = dk.astype(out.dtype)
             out[1, :, cols] = dv.astype(out.dtype)
+            return carry
+
+        lax.fori_loop(0, HK, one, 0)
 
     def pick(a, b, d, e):
         return jnp.where(z == 0, a, jnp.where(z == 1, b, jnp.where(z == 2, d, e)))
@@ -551,49 +509,9 @@
             xsend.at[o, h], xrecv.at[o, h], rx_s.at[h, o], rx_r.at[h, o], partner
         )
 
-    near = (None, (z == 1) | (z == 2), None, None)
-
-    def extra(o):
-        down = order[o] < z
-        i = jnp.where(down, 1, 0)
-        return remote(
-            xsend.at[o, 0], erecv.at[i], ex_s.at[i], ex_r.at[i], jnp.where(down, c - 2, c + 2)
-        )
-
-    def extra_in(i):
-        return remote(erecv.at[i], erecv.at[i], ex_s.at[i], ex_r.at[i], partner)
-
     def phase(o):
         terms(2 * order[o] + 1 - x, xsend.at[o])
-        if o == 2:
-            extra(2).start()
-        elif o == 1:
-
-            @pl.when(near[1])
-            def _():
-                extra(1).start()
-
-            @pl.when(jnp.logical_not(near[1]))
-            def _():
-                cross(0, 1).start()
-
-        elif o == 3:
-
-            @pl.when(z > 0)
-            def _():
-                extra_in(0).wait_recv()
-                both = xsend[3, 0].astype(jnp.float32) + erecv[0].astype(jnp.float32)
-                xsend[3, 0] = both.astype(jnp.bfloat16)
-
-            @pl.when(z < ROWS - 1)
-            def _():
-                extra_in(1).wait_recv()
-                both = xsend[3, 0].astype(jnp.float32) + erecv[1].astype(jnp.float32)
-                xsend[3, 0] = both.astype(jnp.bfloat16)
-
-            cross(0, 3).start()
-        else:
-            cross(0, 0).start()
+        cross(0, o).start()
         cross(1, o).start()
         terms(2 * order[o] + x, acc.at[o])
 
@@ -612,14 +530,8 @@
         down = order[o] < z
         fed = (down & (z < ROWS - 1)) | (jnp.logical_not(down) & (z > 0))
 
-        def add_crossed():
-            cross(h, o).wait_recv()
-            acc[o, h] = acc[o, h] + xrecv[o, h].astype(jnp.float32)
-
-        if h == 1 or o == 0:
-            add_crossed()
-        elif o == 1:
-            pl.when(jnp.logical_not(near[1]))(add_crossed)
+        cross(h, o).wait_recv()
+        acc[o, h] = acc[o, h] + xrecv[o, h].astype(jnp.float32)
 
         @pl.when(fed)
         def _():
@@ -629,16 +541,10 @@
         csend[o, h] = acc[o, h].astype(jnp.bfloat16)
         chain(h, o).start()
 
-    edge = (z == 0) | (z == ROWS - 1)
     phase(0)
     phase(1)
     pass_on(0, 0)
     phase(2)
-
-    @pl.when(edge)
-    def _():
-        pass_on(2, 0)
-
     pass_on(0, 1)
     phase(3)
 
@@ -667,10 +573,7 @@
         store.start()
     pass_on(1, 1)
 
-    @pl.when(jnp.logical_not(edge))
-    def _():
-        pass_on(2, 0)
-
+    pass_on(2, 0)
     pass_on(2, 1)
     last = ROWS - 1
     for h, out in ((0, gk_ref), (1, gv_ref)):
@@ -691,36 +594,10 @@
 
     for store in stores:
         store.wait()
-    across(0, z).wait_send()
     for h in (0, 1):
-        cross(h, 0).wait_send()
-        cross(h, 3).wait_send()
-    cross(1, 1).wait_send()
-    cross(1, 2).wait_send()
-    extra(2).wait_send()
-
-    @pl.when(near[1])
-    def _():
-        extra(1).wait_send()
-
-    @pl.when(jnp.logical_not(near[1]))
-    def _():
-        cross(0, 1).wait_send()
-
-    @pl.when(z < ROWS - 1)
-    def _():
-        beside(True).wait_send()
-
-    @pl.when(z > 0)
-    def _():
-        beside(False).wait_send()
-
-    for zz in range(ROWS):
-        across(1, zz).wait_send()
-
-        @pl.when(jnp.abs(z - zz) > 1)
-        def _():
-            across(0, zz).wait_send()
+        for zz in range(ROWS):
+            across(h, zz).wait_send()
+            cross(h, zz).wait_send()
 
     for h in (0, 1):
         for o in range(ROWS - 1):
@@ -737,15 +614,18 @@
 
 
 def copy_kernel(*refs):
-    sems = refs[-1]
-    count = len(refs) // 2
-    copies = [
-        pltpu.make_async_copy(refs[i], refs[count + i], sems.at[i]) for i in range(count)
-    ]
-    for copy in copies:
-        copy.start()
-    for copy in copies:
-        copy.wait()
+    count = 4
+    ins, outs, held = (refs[i * count : (i + 1) * count] for i in range(3))
+    sems = refs[3 * count]
+    loads = [pltpu.make_async_copy(ins[i], held[i], sems.at[0, i]) for i in range(count)]
+    stores = [pltpu.make_async_copy(held[i], outs[i], sems.at[1, i]) for i in range(count)]
+    for load in loads:
+        load.start()
+    for load, store in zip(loads, stores):
+        load.wait()
+        store.start()
+    for store in stores:
+        store.wait()
 
 
 def dense(queries, keys, values, grad_out, positions):
@@ -790,7 +670,6 @@
             pltpu.VMEM((ROWS, 2, TOK, key_width), bf16),
             pltpu.VMEM((ROWS - 1, 2, TOK, key_width), bf16),
             pltpu.VMEM((ROWS + 1, 2, TOK, key_width), bf16),
-            pltpu.VMEM((2, TOK, key_width), bf16),
             dma((4,)),
             dma((2,)),
             dma((2, ROWS)),
@@ -799,14 +678,10 @@
             dma((2, ROWS - 1)),
             dma((2, ROWS - 1)),
             dma((2, ROWS - 1)),
-            dma((2,)),
-            dma((2,)),
             dma((2, ROWS)),
             dma((2, ROWS)),
             dma((2, ROWS - 1)),
             dma((2, ROWS + 1)),
-            dma((2,)),
-            dma((2,)),
         ],
         compiler_params=pltpu.CompilerParams(
             collective_id=0, has_side_effects=True, vmem_limit_bytes=56 * 1024 * 1024
@@ -817,7 +692,7 @@
         out_shape=shapes,
         in_specs=[anywhere] * 4,
         out_specs=[anywhere] * 4,
-        scratch_shapes=[dma((4,))],
+        scratch_shapes=[pltpu.VMEM(a.shape, bf16) for a in shapes] + [dma((2, 4))],
     )(*results)
 
 

time: 102 us -> 57.5 us (0.56)
  Pallas kernels: 101 us -> 56.7 us
    pallas_call x1, Pallas kernels: 40.8 us -> 2.16 us  [dense(): pl.pallas_call(copy_kernel, out_shape=shapes, in_specs=[anywhere] * 4, ou...]
    pallas_call x1, Pallas kernels: 60.4 us -> 54.6 us  [dense(): pl.pallas_call(dense_kernel, out_shape=shapes, in_specs=[vmem] + [anywher...]
where the time goes in v4:
time: 57.5 us; the launch traced here: 57.4 us
  Pallas kernels  56.7 us (99%)
  between operations  0.64 us (1%)
    pallas_call x1, Pallas kernels, dense(): pl.pallas_call(dense_kernel, out_shape=shapes, in_specs=[vmem] + [anywher...  54.6 us
    pallas_call x1, Pallas kernels, dense(): pl.pallas_call(copy_kernel, out_shape=shapes, in_specs=[anywhere] * 4, ou...  2.16 us

profile of v4, /device:TPU:0, one launch (start us, length us, event | category | flops | bytes accessed | tf_op | source)
XLA Modules:
  0.0 57.4 jit_solution(17400618420466123679)
XLA Ops:
  0.6 54.6 %shard_map.84 = (bf16[128,2048]{1,0:T(8,128)(2,1)}, bf16[128,2048]{1,0:T(8,128)(2,1)}, bf16[128,512]{1,0:T(8,128)(2,1)}, bf16[128,512]{1,0:T(8,128)(2,1)}) custom-call(s32[1,256]{1,0:T(1,128)} %bitcast.1, bf16[128,2048]{1,0:T(8,128)(2,1)} %q_in.1, bf16[128,512]{1,0:T(8,128)(2,1)} %k_in.1, bf16[128,512]{1,0:T(8,128)(2,1)} %v_in.1, bf16[128,2048]{1,0:T(8,128)(2,1)} %g_in.1), custom_call_target="tpu_custom_call" | custom-call | tf_op jit(solution)/shard_map/pallas_call | solution.py:645
  55.2 2.2 %shard_map.85 = (bf16[128,2048]{1,0:T(8,128)(2,1)}, bf16[128,2048]{1,0:T(8,128)(2,1)}, bf16[128,512]{1,0:T(8,128)(2,1)}, bf16[128,512]{1,0:T(8,128)(2,1)}) custom-call(bf16[128,2048]{1,0:T(8,128)(2,1)} %get-tuple-element.8.refs_0_, bf16[128,2048]{1,0:T(8,128)(2,1)} %get-tuple-element.9.refs_1_, bf16[128,512]{1,0:T(8,128)(2,1)} %get-tuple-element.10.refs_2_, ...), custom_call_target="tpu_custom_call" | custom-call | tf_op jit(solution)/shard_map/pallas_call | solution.py:690
